TPU v7x, 128 devices: a whole 4x4x4 slice. The times are simulated.
128 devices in a mesh: dyn: 16 (over y, x), col: 8 (over z, core).
Axes of the slice: x: 4, y: 4, z: 4, core: 2. Of those that a mesh axis runs over, the one named last changes fastest.
Arguments:
- tracer: bfloat16 [1024, 768, 128], P('dyn', 'col'), may hold values from -6 to 6
- temper: bfloat16 [1024, 768, 128], P('dyn', 'col'), may hold values from -6 to 6
- winds: bfloat16 [2, 1024, 768, 128], P(None, 'dyn', 'col'), may hold values from -6 to 6
- owners: int32 [196608, 1], P(('dyn', 'col')), may hold values from 0 to 127; in each aligned block of 1536 rows (0 to 1535, 1536 to 3071, ...) at most 24 rows name the same one
- classes: int32 [196608], P(('dyn', 'col')), may hold values from 0 to 3
- aerosol: bfloat16 [128, 3072, 2048], P(('dyn', 'col')), may hold values from 0.25 to 4
- band_in: bfloat16 [256, 2048], replicated, may hold values from -0.375 to 0.375
- band_out: bfloat16 [2048, 256], replicated, may hold values from -0.125 to 0.125
Outputs:
- tracer_new: bfloat16 [1024, 768, 128], P('dyn', 'col')
- column_tend: bfloat16 [196608, 256], P(('dyn', 'col'))
Inputs may be any that keep to these rules, and one draw needn't show every extreme that they name: `owners`: among the 1536 columns of one device no owner is named more than 24 times, a bound that some block reaches.
All inputs are finite; a program needn't handle non-finite values.
Results may differ from a plain program's by a relative error of at most 0.005.
Values may be sent and summed in bfloat16 or wider, within the bound.
No kernel may reach another device: no remote copies, remote signals or barrier semaphores. Data moves between devices by JAX's collectives and lax.ppermute only.
A program may use at most 128 MiB of HBM per device.

v0:
```python
import math

import jax
import jax.numpy as jnp
import numpy as np
from jax import lax
from jax.sharding import PartitionSpec as P

STEP_SIZE = 0.1
BLOCK_ROWS = 512


def extended(shard, sides, width):
    for axis, dim in sides:
        size, length = (lax.axis_size(axis), shard.shape[dim])
        up = [(i, (i + 1) % size) for i in range(size)]
        down = [(j, i) for i, j in up]
        last = lax.slice_in_dim(shard, length - width, length, axis=dim)
        first = lax.slice_in_dim(shard, 0, width, axis=dim)
        before = lax.ppermute(last, axis, up)
        after = lax.ppermute(first, axis, down)
        shard = jnp.concatenate([before, shard, after], axis=dim)
    return shard


def lagrange_tables():
    points = np.array([-1.0, -1.0 / math.sqrt(5.0), 1.0 / math.sqrt(5.0), 1.0])
    products = np.array(
        [
            np.prod(
                [points[row_at] - points[inner_at] for inner_at in range(4) if inner_at != row_at]
            )
            for row_at in range(4)
        ]
    )
    derivative = np.zeros((4, 4))
    for row_at in range(4):
        for col_at in range(4):
            if row_at == col_at:
                derivative[row_at, col_at] = np.sum(
                    [
                        1.0 / (points[row_at] - points[inner_at])
                        for inner_at in range(4)
                        if inner_at != row_at
                    ]
                )
            else:
                derivative[row_at, col_at] = products[row_at] / (
                    products[col_at] * (points[row_at] - points[col_at])
                )
    average = np.array([[1.0 / 6.0, 5.0 / 6.0, 0.0, 0.0], [0.0, 0.0, 5.0 / 6.0, 1.0 / 6.0]])
    return (derivative, average)


def apply_small(matrix, field, axis):
    pieces = [lax.index_in_dim(field, inner_at, axis, keepdims=True) for inner_at in range(4)]
    outputs = []
    for row_at in range(matrix.shape[0]):
        total = None
        for inner_at in range(4):
            weight = float(matrix[row_at, inner_at])
            if weight != 0.0:
                term = weight * pieces[inner_at]
                total = term if total is None else total + term
        outputs.append(total)
    return jnp.concatenate(outputs, axis=axis)


def tendency(state, wind_pair, derivative):
    rows_x, cols_y, levels = state.shape
    along_x = apply_small(derivative, state.reshape(rows_x // 4, 4, cols_y, levels), 1).reshape(
        state.shape
    )
    along_y = apply_small(derivative, state.reshape(rows_x, cols_y // 4, 4, levels), 2).reshape(
        state.shape
    )
    return -(wind_pair[0] * along_x + wind_pair[1] * along_y)


def assemble_padded(padded, dimension):
    extent = padded.shape[dimension] - 2
    middle = lax.slice_in_dim(padded, 1, extent + 1, axis=dimension)
    forward = lax.slice_in_dim(padded, 2, extent + 2, axis=dimension)
    backward = lax.slice_in_dim(padded, 0, extent, axis=dimension)
    layout = [1, 1, 1]
    layout[dimension] = extent
    position = (jnp.arange(extent) % 4).reshape(layout)
    return jnp.where(
        position == 3,
        0.5 * (middle + forward),
        jnp.where(position == 0, 0.5 * (middle + backward), middle),
    )


def remap(field, average):
    rows_x, cols_y, levels = field.shape
    blocks = field.reshape(rows_x // 4, 4, cols_y // 4, 4, levels)
    cells = apply_small(average, apply_small(average, blocks, 1), 3)
    return cells.reshape(rows_x // 2, cols_y // 2, levels)


def radiate(state, cost_class, optical, band_in, band_out, band_count):
    optical_depth = jnp.dot(state, band_in, preferred_element_type=jnp.float32)
    optical_depth = optical_depth.reshape(state.shape[0], band_count, -1)
    factors = optical.astype(jnp.float32).reshape(state.shape[0], band_count, -1)
    active = jnp.arange(band_count)[None, :] < (cost_class[:, None] + 1) * band_count // 4
    thinned = jnp.exp(-jax.nn.softplus(optical_depth) * factors) * active[:, :, None]
    thinned = thinned.astype(jnp.bfloat16).reshape(state.shape[0], -1)
    return jnp.dot(thinned, band_out, preferred_element_type=jnp.float32).astype(jnp.bfloat16)


def radiate_blocks(state, cost_class, optical, band_in, band_out, band_count):
    row_count = state.shape[0]
    block = math.gcd(row_count, BLOCK_ROWS)
    count = row_count // block

    def one_block(pieces):
        return radiate(pieces[0], pieces[1], pieces[2], band_in, band_out, band_count)

    result = lax.map(
        one_block,
        (
            state.reshape(count, block, -1),
            cost_class.reshape(count, block),
            optical.reshape(count, block, -1),
        ),
    )
    return result.reshape(row_count, -1)


def shards(tracer, temper, winds, owners, classes, aerosol, band_in, band_out):
    derivative, average = lagrange_tables()
    band_count = band_in.shape[1] // tracer.shape[2]
    tend = tendency(tracer.astype(jnp.float32), winds.astype(jnp.float32), derivative)
    padded = extended(tend, (("dyn", 0), ("col", 1)), 1)
    assembled = assemble_padded(assemble_padded(padded, 0), 1)
    tracer_new = (tracer.astype(jnp.float32) + STEP_SIZE * assembled).astype(jnp.bfloat16)
    cells_tracer = remap(tracer_new.astype(jnp.float32), average)
    cells_temper = remap(temper.astype(jnp.float32), average)
    joined = jnp.concatenate([cells_tracer, cells_temper], axis=2).astype(jnp.bfloat16)
    width_two = joined.shape[2]
    column_state = joined.reshape(-1, width_two)
    devices = lax.axis_size(("dyn", "col"))
    capacity = aerosol.shape[1] // devices
    destination = owners[:, 0]
    onehot = (destination[:, None] == jnp.arange(devices, dtype=jnp.int32)[None, :]).astype(
        jnp.int32
    )
    earlier = jnp.cumsum(onehot, axis=0) - onehot
    slot = jnp.sum(earlier * onehot, axis=1)
    target = destination * capacity + slot
    outgoing = jnp.zeros((devices * capacity, width_two), jnp.bfloat16).at[target].set(column_state)
    class_out = (
        jnp.zeros((devices * capacity,), jnp.bfloat16).at[target].set(classes.astype(jnp.bfloat16))
    )
    arrived, arrived_class = (
        lax.all_to_all(
            outgoing.reshape(devices, capacity, width_two),
            ("dyn", "col"),
            split_axis=0,
            concat_axis=0,
            tiled=True,
        ),
        lax.all_to_all(
            class_out.reshape(devices, capacity),
            ("dyn", "col"),
            split_axis=0,
            concat_axis=0,
            tiled=True,
        ),
    )
    class_whole = arrived_class.reshape(-1).astype(jnp.int32)
    result = radiate_blocks(
        arrived.reshape(-1, width_two), class_whole, aerosol[0], band_in, band_out, band_count
    )
    returned = lax.all_to_all(
        result.reshape(devices, capacity, width_two),
        ("dyn", "col"),
        split_axis=0,
        concat_axis=0,
        tiled=True,
    )
    column_tend = returned.reshape(-1, width_two)[target]
    return (tracer_new, column_tend)


def solution(mesh):
    return jax.shard_map(
        shards,
        mesh=mesh,
        in_specs=(
            P("dyn", "col", None),
            P("dyn", "col", None),
            P(None, "dyn", "col", None),
            P(("dyn", "col"), None),
            P(("dyn", "col")),
            P(("dyn", "col"), None, None),
            P(),
            P(),
        ),
        out_specs=(P("dyn", "col", None), P(("dyn", "col"), None)),
        check_vma=False,
    )
```

profile of v0, /device:TPU:1, one launch (start us, length us, event | category | flops | bytes accessed | tf_op | source)
XLA Modules:
  0.0 216.3 jit_solution(9259119033698338330)
XLA Ops:
  0.6 1.9 copy_convert_fusion.1
  3.0 2.2 %multiply_add_fusion.3 = (f32[64,24,1,128]{3,1,2,0:T(8,128)S(1)}, f32[64,24,1,128]{3,1,2,0:T(8,128)S(1)}, f32[64,24,1,128]{3,1,2,0:T(8,128)S(1)}, f32[64,24,1,128]{3,1,2,0:T(8,128)S(1)}) fusion(f32[64,24,1,128]{3,0,2,1:T(8,128)S(1)} %get-tuple-element.159, f32[64,24,1,128]{3,0,2,1:T(8,128)S(1)} %get-tuple-element.157, ...), kind=kLoop, calls=%fused_computation.91 | loop fusion | flops 5505024 | bytes 6291456 | tf_op jit(solution)/shard_map/add | solution.py:64
  7.3 7.4 %multiply_add_fusion.7 = (f32[16,1,96,128]{3,1,0,2:T(1,128)S(1)}, f32[16,1,96,128]{3,1,0,2:T(1,128)S(1)}, f32[16,1,96,128]{3,1,0,2:T(1,128)S(1)}, f32[16,1,96,128]{3,1,0,2:T(1,128)S(1)}) fusion(f32[16,4,96,128]{3,1,0,2:T(4,128)S(1)} %bitcast.81), kind=kLoop, calls=%fused_computation.95 | loop fusion | flops 5505024 | bytes 6291456 | tf_op jit(solution)/shard_map/add | solution.py:64
  15.7 3.0 %pad_maximum_fusion.1 = f32[16,4,96,128]{3,1,0,2:T(4,128)S(1)} fusion(f32[16,1,96,128]{3,1,0,2:T(1,128)S(1)} %get-tuple-element.163, f32[16,1,96,128]{3,1,0,2:T(1,128)S(1)} %get-tuple-element.162, f32[16,1,96,128]{3,1,0,2:T(1,128)S(1)} %get-tuple-element.161, f32[16,1,96,128]{3,1,0,2:T(1,128)S(1)} %get-tuple-element.160), kind=kLoop, calls=%fused_computation.48 | loop fusion | flops 2359296 | bytes 6291456 | tf_op jit(solution)/shard_map/concatenate | solution.py:66
  18.7 1.9 fusion.26
  20.7 2.3 %collective-permute-start = (f32[1,96,128]{2,0,1:T(1,128)S(1)}, f32[1,96,128]{2,0,1:T(1,128)S(1)}, u32[]{:S(2)}, u32[]{:S(2)}) collective-permute-start(f32[1,96,128]{2,0,1:T(1,128)S(1)} %get-tuple-element.150), channel_id=1, source_target_pairs={{0,8},{8,16},{16,24},{24,32},{32,40},{40,48},{48,56},{56,64},{64,7... | collective-permute-start | bytes 147464 | tf_op jit(solution)/shard_map/ppermute | solution.py:20
  23.0 3.8 %collective-permute-start.1 = (f32[1,96,128]{2,0,1:T(1,128)S(1)}, f32[1,96,128]{2,0,1:T(1,128)S(1)}, u32[]{:S(2)}, u32[]{:S(2)}) collective-permute-start(f32[1,96,128]{2,0,1:T(1,128)S(1)} %get-tuple-element.151), channel_id=1, source_target_pairs={{8,0},{16,8},{24,16},{32,24},{40,32},{48,40},{56,48},{64,56},{72,6... | collective-permute-start | bytes 147464 | tf_op jit(solution)/shard_map/ppermute | solution.py:21
  30.4 11.1 %scatter_custom_fusion.1 = bf16[3072]{0:T(1024)(128)(2,1)S(1)} fusion(s32[1536]{0:T(1024)S(1)} %fusion.64, bf16[1536]{0:T(1024)(128)(2,1)S(1)} %convert_element_type.69, bf16[]{:T(256)} %constant.155.clone.1), kind=kCustom, calls=%fused_computation.132 | custom fusion | bytes 6146 | tf_op jit(solution)/shard_map/scatter | solution.py:154
  42.2 8.2 %all-to-all-start.1 = ((bf16[128,1,24]{2,1,0:T(2,128)(2,1)}), bf16[128,1,24]{2,1,0:T(2,128)(2,1)}, u32[]{:S(2)}, u32[]{:S(2)}) async-start(bf16[128,1,24]{2,1,0:T(2,128)(2,1)} %all_to_all.16), calls=%async_computation.1 | async-start | bytes 131072 | tf_op jit(solution)/shard_map/all_to_all | solution.py:164
  55.7 2.7 %collective-permute-done.3 = f32[66,1,128]{2,0,1:T(8,128)S(1)} collective-permute-done((f32[66,1,128]{2,0,1:T(8,128)S(1)}, f32[66,1,128]{2,0,1:T(8,128)S(1)}, u32[]{:S(2)}, u32[]{:S(2)}) %collective-permute-start.3) | collective-permute-done | bytes 33824 | tf_op jit(solution)/shard_map/ppermute | solution.py:21
  61.2 2.9 %fusion.22 = bf16[64,96,128]{2,0,1:T(8,128)(2,1)S(1)} fusion(f32[64,98,128]{2,0,1:T(8,128)S(1)} %fusion.15, pred[96]{0:T(512)(128)(4,1)S(1)} %get-tuple-element.174, pred[96]{0:T(512)(128)(4,1)S(1)} %get-tuple-element.175, bf16[64,96,128]{2,1,0:T(8,128)(2,1)S(1)} %copy-done.3), kind=kLoop, calls=%fused_computation.39 | loop fusion | flops 7864320 | bytes 12583104 | tf_op jit(solution)/shard_map/convert_element_type | solution.py:137
  66.2 8.5 %scatter_custom_fusion = bf16[3072,256]{1,0:T(8,128)(2,1)} fusion(s32[1536]{0:T(1024)S(1)} %fusion.64, bf16[1536,128]{1,0:T(8,128)(2,1)S(1)} %bitcast.87, bf16[]{:T(256)} %constant.166, bf16[1536,128]{1,0:T(8,128)(2,1)S(1)} %bitcast.88, bf16[]{:T(256)} %constant.155.clone.1), kind=kCustom, calls=%fused_computation.67 | custom fusion | flops 1572864 | bytes 2359300 | tf_op jit(solution)/shard_map/scatter | solution.py:152
  74.6 8.8 %all-to-all-start = ((bf16[128,24,256]{2,1,0:T(8,128)(2,1)}), bf16[128,24,256]{2,1,0:T(8,128)(2,1)S(1)}, u32[]{:S(2)}, u32[]{:S(2)}) async-start(bf16[128,24,256]{2,1,0:T(8,128)(2,1)} %bitcast.22), calls=%async_computation | async-start | bytes 3145728 | tf_op jit(solution)/shard_map/all_to_all | solution.py:157
  83.4 2.3 %copy.47 = bf16[256,2048]{0,1:T(8,128)(2,1)} copy(bf16[256,2048]{1,0:T(8,128)(2,1)} %param.16) | data formatting | bytes 2097152 | tf_op jit(solution)/shard_map/while | solution.py:120
  86.8 21.3 %all-to-all-done = bf16[128,24,256]{2,1,0:T(8,128)(2,1)S(1)} async-done(((bf16[128,24,256]{2,1,0:T(8,128)(2,1)}), bf16[128,24,256]{2,1,0:T(8,128)(2,1)S(1)}, u32[]{:S(2)}, u32[]{:S(2)}) %all-to-all-start) | async-done | bytes 1572896 | tf_op jit(solution)/shard_map/all_to_all | solution.py:157
  108.1 73.2 %while.12 = (s32[]{:T(128)}, bf16[6,512,256]{2,1,0:T(8,128)(2,1)}, bf16[6,512,256]{2,1,0:T(8,128)(2,1)S(1)}, bf16[256,2048]{0,1:T(8,128)(2,1)}, bf16[6,512,2048]...) while((s32[]{:T(128)}, bf16[6,512,256]{2,1,0:T(8,128)(2,1)}, ...), condition=%wide.region_6.7_spmd, body=%wide.region_5.6_spmd.sunk | while | flops 1085432320 | bytes 29961364 | solution.py:120
  111.0 2.5 %copy.108 = bf16[1,512,2048]{1,2,0:T(8,128)(2,1)} copy(bf16[1,512,2048]{2,1,0:T(8,128)(2,1)S(1)} %constant_dynamic-slice_fusion.2) | data formatting | bytes 4194304 | tf_op jit(solution)/shard_map/while/body/jit(dynamic_index_in_dim)/dynamic_slice | solution.py:120
  113.5 5.3 %fusion.86 = bf16[512,16,128]{0,2,1:T(8,128)(2,1)S(1)} fusion(bf16[512,16,128]{0,2,1:T(8,128)(2,1)} %bitcast.77, f32[512,16]{0,1:T(8,128)S(1)} %fusion.85, bf16[16,128,256]{2,1,0:T(8,128)(2,1)} %bitcast.89, bf16[6,512,256]{2,1,0:T(8,128)(2,1)} %copy-done.6, s32[]{:T(128)} %get-tuple-element.229), kind=kOutput, calls=%fused_computation.8.clone.1 | convolution fusion | flops 548405248 | bytes 5538304 | tf_op jit(solution)/shard_map/while/body/eval_jaxpr/dot_general | solution.py:103
  123.2 2.5 %copy.108 = bf16[1,512,2048]{1,2,0:T(8,128)(2,1)} copy(bf16[1,512,2048]{2,1,0:T(8,128)(2,1)S(1)} %constant_dynamic-slice_fusion.2) | data formatting | bytes 4194304 | tf_op jit(solution)/shard_map/while/body/jit(dynamic_index_in_dim)/dynamic_slice | solution.py:120
  125.7 5.3 %fusion.86 = bf16[512,16,128]{0,2,1:T(8,128)(2,1)S(1)} fusion(bf16[512,16,128]{0,2,1:T(8,128)(2,1)} %bitcast.77, f32[512,16]{0,1:T(8,128)S(1)} %fusion.85, bf16[16,128,256]{2,1,0:T(8,128)(2,1)} %bitcast.89, bf16[6,512,256]{2,1,0:T(8,128)(2,1)} %copy-done.6, s32[]{:T(128)} %get-tuple-element.229), kind=kOutput, calls=%fused_computation.8.clone.1 | convolution fusion | flops 548405248 | bytes 5538304 | tf_op jit(solution)/shard_map/while/body/eval_jaxpr/dot_general | solution.py:103
  135.4 2.5 %copy.108 = bf16[1,512,2048]{1,2,0:T(8,128)(2,1)} copy(bf16[1,512,2048]{2,1,0:T(8,128)(2,1)S(1)} %constant_dynamic-slice_fusion.2) | data formatting | bytes 4194304 | tf_op jit(solution)/shard_map/while/body/jit(dynamic_index_in_dim)/dynamic_slice | solution.py:120
  137.9 5.2 %fusion.86 = bf16[512,16,128]{0,2,1:T(8,128)(2,1)S(1)} fusion(bf16[512,16,128]{0,2,1:T(8,128)(2,1)} %bitcast.77, f32[512,16]{0,1:T(8,128)S(1)} %fusion.85, bf16[16,128,256]{2,1,0:T(8,128)(2,1)} %bitcast.89, bf16[6,512,256]{2,1,0:T(8,128)(2,1)} %copy-done.6, s32[]{:T(128)} %get-tuple-element.229), kind=kOutput, calls=%fused_computation.8.clone.1 | convolution fusion | flops 548405248 | bytes 5538304 | tf_op jit(solution)/shard_map/while/body/eval_jaxpr/dot_general | solution.py:103
  147.6 2.5 %copy.108 = bf16[1,512,2048]{1,2,0:T(8,128)(2,1)} copy(bf16[1,512,2048]{2,1,0:T(8,128)(2,1)S(1)} %constant_dynamic-slice_fusion.2) | data formatting | bytes 4194304 | tf_op jit(solution)/shard_map/while/body/jit(dynamic_index_in_dim)/dynamic_slice | solution.py:120
  150.1 5.2 %fusion.86 = bf16[512,16,128]{0,2,1:T(8,128)(2,1)S(1)} fusion(bf16[512,16,128]{0,2,1:T(8,128)(2,1)} %bitcast.77, f32[512,16]{0,1:T(8,128)S(1)} %fusion.85, bf16[16,128,256]{2,1,0:T(8,128)(2,1)} %bitcast.89, bf16[6,512,256]{2,1,0:T(8,128)(2,1)} %copy-done.6, s32[]{:T(128)} %get-tuple-element.229), kind=kOutput, calls=%fused_computation.8.clone.1 | convolution fusion | flops 548405248 | bytes 5538304 | tf_op jit(solution)/shard_map/while/body/eval_jaxpr/dot_general | solution.py:103
  159.8 2.5 %copy.108 = bf16[1,512,2048]{1,2,0:T(8,128)(2,1)} copy(bf16[1,512,2048]{2,1,0:T(8,128)(2,1)S(1)} %constant_dynamic-slice_fusion.2) | data formatting | bytes 4194304 | tf_op jit(solution)/shard_map/while/body/jit(dynamic_index_in_dim)/dynamic_slice | solution.py:120
  162.3 5.2 %fusion.86 = bf16[512,16,128]{0,2,1:T(8,128)(2,1)S(1)} fusion(bf16[512,16,128]{0,2,1:T(8,128)(2,1)} %bitcast.77, f32[512,16]{0,1:T(8,128)S(1)} %fusion.85, bf16[16,128,256]{2,1,0:T(8,128)(2,1)} %bitcast.89, bf16[6,512,256]{2,1,0:T(8,128)(2,1)} %copy-done.6, s32[]{:T(128)} %get-tuple-element.229), kind=kOutput, calls=%fused_computation.8.clone.1 | convolution fusion | flops 548405248 | bytes 5538304 | tf_op jit(solution)/shard_map/while/body/eval_jaxpr/dot_general | solution.py:103
  172.0 2.5 %copy.108 = bf16[1,512,2048]{1,2,0:T(8,128)(2,1)} copy(bf16[1,512,2048]{2,1,0:T(8,128)(2,1)S(1)} %constant_dynamic-slice_fusion.2) | data formatting | bytes 4194304 | tf_op jit(solution)/shard_map/while/body/jit(dynamic_index_in_dim)/dynamic_slice | solution.py:120
  174.5 5.3 %fusion.86 = bf16[512,16,128]{0,2,1:T(8,128)(2,1)S(1)} fusion(bf16[512,16,128]{0,2,1:T(8,128)(2,1)} %bitcast.77, f32[512,16]{0,1:T(8,128)S(1)} %fusion.85, bf16[16,128,256]{2,1,0:T(8,128)(2,1)} %bitcast.89, bf16[6,512,256]{2,1,0:T(8,128)(2,1)} %copy-done.6, s32[]{:T(128)} %get-tuple-element.229), kind=kOutput, calls=%fused_computation.8.clone.1 | convolution fusion | flops 548405248 | bytes 5538304 | tf_op jit(solution)/shard_map/while/body/eval_jaxpr/dot_general | solution.py:103
  181.3 4.8 %all-to-all-start.2 = ((bf16[128,24,256]{2,1,0:T(8,128)(2,1)}), bf16[128,24,256]{2,1,0:T(8,128)(2,1)S(1)}, u32[]{:S(2)}, u32[]{:S(2)}) async-start(bf16[128,24,256]{2,1,0:T(8,128)(2,1)} %bitcast.25), calls=%async_computation.2 | async-start | bytes 3145728 | tf_op jit(solution)/shard_map/all_to_all | solution.py:176
  186.1 2.2 copy.49
  188.3 22.6 %all-to-all-done.2 = bf16[128,24,256]{2,1,0:T(8,128)(2,1)S(1)} async-done(((bf16[128,24,256]{2,1,0:T(8,128)(2,1)}), bf16[128,24,256]{2,1,0:T(8,128)(2,1)S(1)}, u32[]{:S(2)}, u32[]{:S(2)}) %all-to-all-start.2) | async-done | bytes 1572896 | tf_op jit(solution)/shard_map/all_to_all | solution.py:176
  210.9 5.4 %gather_fusion = bf16[1536,256]{1,0:T(8,128)(2,1)} fusion(bf16[3072,256]{1,0:T(8,128)(2,1)S(1)} %bitcast.79, s32[2048]{0:T(1024)S(1)} %pad_clamp_fusion), kind=kCustom, calls=%fused_computation | custom fusion | bytes 1579008 | tf_op jit(solution)/shard_map/gather | solution.py:183
  (117 shorter events, 45.3 us)
Async XLA Ops:
  7.2 7.4 %copy-start.5 = (bf16[2,64,96,128]{3,2,1,0:T(8,128)(2,1)S(1)}, bf16[2,64,96,128]{3,2,1,0:T(8,128)(2,1)}, u32[]{:S(2)}) copy-start(bf16[2,64,96,128]{3,2,1,0:T(8,128)(2,1)} %param.12) | copy-start | bytes 9437188
  18.7 8.1 %copy-start.10 = (s32[1536,1]{0,1:T(1,128)S(1)}, s32[1536,1]{0,1:T(1,128)}, u32[]{:S(2)}) copy-start(s32[1536,1]{0,1:T(1,128)} %param.13) | copy-start | bytes 18436
  20.6 9.8 %copy-start.11 = (s32[1536]{0:T(1024)S(1)}, s32[1536]{0:T(1024)}, u32[]{:S(2)}) copy-start(s32[1536]{0:T(1024)} %param.14) | copy-start | bytes 18436
  20.7 32.1 %collective-permute-start = (f32[1,96,128]{2,0,1:T(1,128)S(1)}, f32[1,96,128]{2,0,1:T(1,128)S(1)}, u32[]{:S(2)}, u32[]{:S(2)}) collective-permute-start(f32[1,96,128]{2,0,1:T(1,128)S(1)} %get-tuple-element.150), channel_id=1, source_target_pairs={{0,8},{8,16},{16,24},{24,32},{32,40},{40,48},{48,56},{56,64},{64,7... | collective-permute-start | bytes 147464 | tf_op jit(solution)/shard_map/ppermute | solution.py:20
  23.0 29.8 %collective-permute-start.1 = (f32[1,96,128]{2,0,1:T(1,128)S(1)}, f32[1,96,128]{2,0,1:T(1,128)S(1)}, u32[]{:S(2)}, u32[]{:S(2)}) collective-permute-start(f32[1,96,128]{2,0,1:T(1,128)S(1)} %get-tuple-element.151), channel_id=1, source_target_pairs={{8,0},{16,8},{24,16},{32,24},{40,32},{48,40},{56,48},{64,56},{72,6... | collective-permute-start | bytes 147464 | tf_op jit(solution)/shard_map/ppermute | solution.py:21
  27.2 1.0 copy-start.4
  42.2 32.4 %all-to-all-start.1 = ((bf16[128,1,24]{2,1,0:T(2,128)(2,1)}), bf16[128,1,24]{2,1,0:T(2,128)(2,1)}, u32[]{:S(2)}, u32[]{:S(2)}) async-start(bf16[128,1,24]{2,1,0:T(2,128)(2,1)} %all_to_all.16), calls=%async_computation.1 | async-start | bytes 131072 | tf_op jit(solution)/shard_map/all_to_all | solution.py:164
  52.8 1.8 copy-start.8
  52.8 1.8 copy-start.9
  52.8 2.8 %collective-permute-start.2 = (f32[66,1,128]{2,0,1:T(8,128)S(1)}, f32[66,1,128]{2,0,1:T(8,128)S(1)}, u32[]{:S(2)}, u32[]{:S(2)}) collective-permute-start(f32[66,1,128]{2,0,1:T(8,128)S(1)} %get-tuple-element.144), channel_id=1, source_target_pairs={{0,1},{1,2},{2,3},{3,4},{4,5},{5,6},{6,7},{7,0},{8,9},{9,10},{10,1... | collective-permute-start | bytes 101384 | tf_op jit(solution)/shard_map/ppermute | solution.py:20
  54.6 3.8 %collective-permute-start.3 = (f32[66,1,128]{2,0,1:T(8,128)S(1)}, f32[66,1,128]{2,0,1:T(8,128)S(1)}, u32[]{:S(2)}, u32[]{:S(2)}) collective-permute-start(f32[66,1,128]{2,0,1:T(8,128)S(1)} %get-tuple-element.145), channel_id=1, source_target_pairs={{1,0},{2,1},{3,2},{4,3},{5,4},{6,5},{7,6},{0,7},{9,8},{10,9},{11,1... | collective-permute-start | bytes 101384 | tf_op jit(solution)/shard_map/ppermute | solution.py:21
  59.8 1.4 copy-start.3
  64.1 1.2 copy-start.1
  74.6 33.4 %copy-start = (bf16[2048,256]{1,0:T(8,128)(2,1)S(1)}, bf16[2048,256]{1,0:T(8,128)(2,1)}, u32[]{:S(2)}) copy-start(bf16[2048,256]{1,0:T(8,128)(2,1)} %param.17) | copy-start | bytes 3145732
  74.6 33.4 %all-to-all-start = ((bf16[128,24,256]{2,1,0:T(8,128)(2,1)}), bf16[128,24,256]{2,1,0:T(8,128)(2,1)S(1)}, u32[]{:S(2)}, u32[]{:S(2)}) async-start(bf16[128,24,256]{2,1,0:T(8,128)(2,1)} %bitcast.22), calls=%async_computation | async-start | bytes 3145728 | tf_op jit(solution)/shard_map/all_to_all | solution.py:157
  108.1 1.2 copy-start.6
  118.8 1.5 copy-start.7
  120.3 1.2 copy-start.6
  131.0 1.5 copy-start.7
  132.5 1.2 copy-start.6
  143.2 1.5 copy-start.7
  144.7 1.2 copy-start.6
  155.4 1.5 copy-start.7
  156.8 1.2 copy-start.6
  167.6 1.5 copy-start.7
  169.1 1.2 copy-start.6
  179.8 1.5 copy-start.7
  181.3 4.8 %copy-start.2 = (bf16[64,96,128]{2,0,1:T(8,128)(2,1)S(1)}, bf16[64,96,128]{2,0,1:T(8,128)(2,1)}, u32[]{:S(2)}) copy-start(bf16[64,96,128]{2,0,1:T(8,128)(2,1)} %copy-done.1) | copy-start | bytes 4718596
  181.3 29.6 %all-to-all-start.2 = ((bf16[128,24,256]{2,1,0:T(8,128)(2,1)}), bf16[128,24,256]{2,1,0:T(8,128)(2,1)S(1)}, u32[]{:S(2)}, u32[]{:S(2)}) async-start(bf16[128,24,256]{2,1,0:T(8,128)(2,1)} %bitcast.25), calls=%async_computation.2 | async-start | bytes 3145728 | tf_op jit(solution)/shard_map/all_to_all | solution.py:176
where the time goes:
time: 217 us; the launch traced here: 216 us
  local copies, waits for them, and re-layouts  61.9 us (29%)
  waiting for transfers between devices  47.4 us (22%)
  matrix products  40.3 us (19%)
  other arithmetic  36 us (17%)
  starting transfers between devices  29.6 us (14%)
    dot_general x6, matrix products, radiate(): optical_depth = jnp.dot(state, band_in, preferred_element_type=jnp.float32)  31.5 us
    dynamic_slice x12, local copies, waits for them, and re-layouts, radiate_blocks(): lax.map(one_block, (state.reshape(count, block, -1), cost_class.reshape(c...  25.6 us
    all_to_all x1, waiting for transfers between devices, shards(): lax.all_to_all(result.reshape(devices, capacity, width_two), ('dyn', 'col...  22.6 us
    all_to_all x1, waiting for transfers between devices, shards(): lax.all_to_all(outgoing.reshape(devices, capacity, width_two), ('dyn', 'c...  21.3 us
    scatter x1, local copies, waits for them, and re-layouts, shards(): jnp.zeros((devices * capacity,), jnp.bfloat16).at[target]  11.1 us
    add x5, other arithmetic, apply_small(): total = term if total is None else total + term  10.3 us
    dot_general x6, matrix products, radiate(): jnp.dot(thinned, band_out, preferred_element_type=jnp.float32)  8.78 us
    all_to_all x1, starting transfers between devices, shards(): lax.all_to_all(outgoing.reshape(devices, capacity, width_two), ('dyn', 'c...  8.75 us
  transfers between devices with their start and end apart: 7, of which 4 were waited for; matrix products, arithmetic and copies ran while one was open for 17% of the time, Pallas kernels for 0%

commit v1 on v0

v1 whole, which is shorter than its diff:
```python
import functools
import math

import jax
import jax.numpy as jnp
import numpy as np
from jax import lax
from jax.experimental import pallas as pl
from jax.experimental.pallas import tpu as pltpu
from jax.sharding import PartitionSpec as P

STEP_SIZE = 0.1
F32, BF16, I32 = jnp.float32, jnp.bfloat16, jnp.int32
MIB = 1024 * 1024


def lagrange_tables():
    points = np.array([-1.0, -1.0 / math.sqrt(5.0), 1.0 / math.sqrt(5.0), 1.0])
    products = np.array(
        [np.prod([points[r] - points[k] for k in range(4) if k != r]) for r in range(4)]
    )
    derivative = np.zeros((4, 4))
    for r in range(4):
        for c in range(4):
            if r == c:
                derivative[r, c] = np.sum(
                    [1.0 / (points[r] - points[k]) for k in range(4) if k != r]
                )
            else:
                derivative[r, c] = products[r] / (products[c] * (points[r] - points[c]))
    average = np.array([[1.0 / 6.0, 5.0 / 6.0, 0.0, 0.0], [0.0, 0.0, 5.0 / 6.0, 1.0 / 6.0]])
    return (derivative, average)


GRAD, PG2 = lagrange_tables()


def combine(weights, pieces):
    total = None
    for weight, piece in zip(weights, pieces):
        if abs(float(weight)) > 1e-12:
            term = float(weight) * piece
            total = term if total is None else total + term
    return total


def cell_pair(nodes):
    halves = [[combine(PG2[a], [nodes[x][k] for x in range(4)]) for k in range(4)] for a in range(2)]
    return [[combine(PG2[b], halves[a]) for b in range(2)] for a in range(2)]


def call(kernel, out_shape, *args, vmem, flops=0, moved=0, **kw):
    return pl.pallas_call(
        kernel,
        out_shape=out_shape,
        compiler_params=pltpu.CompilerParams(vmem_limit_bytes=vmem * MIB),
        cost_estimate=pl.CostEstimate(flops=flops, bytes_accessed=moved, transcendentals=0),
        **kw,
    )(*args)


def full(shape):
    return pl.BlockSpec(shape, lambda *_: (0,) * len(shape))


def edges_kernel(tracer, winds, ex0, ex3, ey0, ey3, xs, xw, ys, yw, line, wind, strip, vstrip, sem):
    nx, ny, lev = tracer.shape
    ne = ny // 4
    copies = []
    for i, (x, x4, y) in enumerate(((0, 0, 0), (nx - 1, nx - 4, ny - 16))):
        copies.append((
            pltpu.make_async_copy(tracer.at[pl.ds(x4, 4)], xs.at[i], sem.at[i, 0]),
            pltpu.make_async_copy(winds.at[:, x], xw.at[i], sem.at[i, 1]),
            pltpu.make_async_copy(tracer.at[:, pl.ds(y, 16)], ys.at[i], sem.at[i, 2]),
            pltpu.make_async_copy(winds.at[:, :, pl.ds(y, 16)], yw.at[i], sem.at[i, 3]),
        ))
    for part in (0, 2):
        for group in copies:
            group[part].start()
            group[part + 1].start()

    for i, (node, out) in enumerate(((0, ex0), (3, ex3))):
        copies[i][0].wait()
        copies[i][1].wait()
        for x in range(4):
            line[pl.ds((4 * i + x) * ny, ny), :] = xs[i, x].astype(F32)
        for h in range(2):
            wind[pl.ds((2 * i + h) * ny, ny), :] = xw[i, h].astype(F32)
        nodes = [
            [line[pl.ds((4 * i + x) * ny + k, ne, stride=4), :] for k in range(4)] for x in range(4)
        ]
        for k in range(4):
            dx = combine(GRAD[node], [nodes[m][k] for m in range(4)])
            dy = combine(GRAD[k], nodes[node])
            u = wind[pl.ds(2 * i * ny + k, ne, stride=4), :]
            v = wind[pl.ds((2 * i + 1) * ny + k, ne, stride=4), :]
            out[pl.ds(k * ne, ne), :] = -(u * dx + v * dy)

    size = nx * 16
    for i, (base, node, out) in enumerate(((0, 0, ey0), (12, 3, ey3))):
        copies[i][2].wait()
        copies[i][3].wait()
        nel = nx // 4
        strip[pl.ds(i * size, size), :] = ys[i].astype(F32).reshape(size, lev)
        for h in range(2):
            vstrip[pl.ds((2 * i + h) * size, size), :] = yw[i, h].astype(F32).reshape(size, lev)
        nodes = [
            [strip[pl.ds(i * size + x * 16 + base + k, nel, stride=64), :] for k in range(4)]
            for x in range(4)
        ]
        for x in range(4):
            dx = combine(GRAD[x], [nodes[m][node] for m in range(4)])
            dy = combine(GRAD[node], nodes[x])
            at = x * 16 + base + node
            u = vstrip[pl.ds(2 * i * size + at, nel, stride=64), :]
            v = vstrip[pl.ds((2 * i + 1) * size + at, nel, stride=64), :]
            out[pl.ds(x, nel, stride=4), :] = -(u * dx + v * dy)


def edges(tracer, winds):
    nx, ny, lev = tracer.shape
    shapes = [(ny, lev)] * 2 + [(nx, lev)] * 2
    return call(
        edges_kernel,
        [jax.ShapeDtypeStruct(s, F32) for s in shapes],
        tracer, winds,
        vmem=53, flops=10**6, moved=3 * 10**6,
        in_specs=[pl.BlockSpec(memory_space=pltpu.HBM)] * 2,
        scratch_shapes=[
            pltpu.VMEM((2, 4, ny, lev), BF16),
            pltpu.VMEM((2, 2, ny, lev), BF16),
            pltpu.VMEM((2, nx, 16, lev), BF16),
            pltpu.VMEM((2, 2, nx, 16, lev), BF16),
            pltpu.VMEM((8 * ny, lev), F32),
            pltpu.VMEM((4 * ny, lev), F32),
            pltpu.VMEM((2 * nx * 16, lev), F32),
            pltpu.VMEM((4 * nx * 16, lev), F32),
            pltpu.SemaphoreType.DMA((2, 4)),
        ],
    )


def sides_kernel(ey0, ey3, xprev, xnext, out0, out3, line):
    nx, lev = ey0.shape
    ny = xprev.shape[0]
    position = lax.broadcasted_iota(I32, (nx, lev), 0) & 3
    for mid, row, out in ((ey0, 0, out0), (ey3, ny - 1, out3)):
        line[pl.ds(7, 1), :] = xprev[pl.ds(row, 1), :]
        line[pl.ds(8, nx), :] = mid[...]
        line[pl.ds(8 + nx, 1), :] = xnext[pl.ds(row, 1), :]
        here = line[pl.ds(8, nx), :]
        back = 0.5 * (here + line[pl.ds(7, nx), :])
        front = 0.5 * (here + line[pl.ds(9, nx), :])
        out[...] = jnp.where(position == 3, front, jnp.where(position == 0, back, here))


def sides(ey0, ey3, xprev, xnext):
    return call(
        sides_kernel,
        [jax.ShapeDtypeStruct(ey0.shape, F32)] * 2,
        ey0, ey3, xprev, xnext,
        vmem=4, flops=10**5, moved=2 * 10**5,
        scratch_shapes=[pltpu.VMEM((ey0.shape[0] + 16, ey0.shape[1]), F32)],
    )


GROUP = 32


def pack(cap, owners_ref, slot_ref, table_ref, values_ref, low_ref, out_ref):
    cols = owners_ref.shape[1]
    lev = out_ref.shape[1]
    rows = GROUP * cap
    each = 2 * cap + 8
    owner = owners_ref[...]
    high = owner // GROUP
    place = (owner - high * GROUP) * cap + slot_ref[...]
    sub = lax.broadcasted_iota(I32, (rows, cols), 0)
    low_ref[...] = (sub == place).astype(F32).astype(BF16)
    none = jnp.zeros((rows, cols), BF16)
    high_all = jnp.broadcast_to(high.astype(F32).astype(BF16), (rows, cols))
    for i in range(table_ref.shape[0] // GROUP):
        hot = jnp.where(high_all == jnp.full((rows, cols), float(i), BF16), low_ref[...], none)
        packed = jnp.dot(hot, values_ref[...], preferred_element_type=F32)
        pieces = []
        for o in range(GROUP):
            line = table_ref[pl.ds(i * GROUP + o, 1), :]
            pieces.append(packed[o * cap : (o + 1) * cap, :lev])
            pieces.append(packed[o * cap : (o + 1) * cap, lev:])
            pieces.append(jnp.broadcast_to(line, (8, lev)))
        out_ref[pl.ds(i * GROUP * each, GROUP * each), :] = jnp.concatenate(pieces, axis=0).astype(BF16)


def cells_of(nodes, cells_ref, row, ne):
    cells = cell_pair(nodes)
    for a in range(2):
        for b in range(2):
            cells_ref[pl.ds(row + a * 2 * ne + b, ne, stride=2), :] = cells[a][b]


def columns_kernel(owners_ref, classes_ref, temper_hbm, slot_ref, table_ref, out_ref,
                   temper_ref, nodes_ref, cells_ref, sem):
    copy = pltpu.make_async_copy(temper_hbm, temper_ref, sem)
    copy.start()
    cols = owners_ref.shape[1]
    nx, ny, lev = temper_ref.shape
    ne = ny // 4
    devices = table_ref.shape[0]
    chunk = 256
    sub = lax.broadcasted_iota(I32, (devices, chunk), 0)
    upper = (
        lax.broadcasted_iota(I32, (chunk, chunk), 0) < lax.broadcasted_iota(I32, (chunk, chunk), 1)
    ).astype(F32).astype(BF16)
    ones = jnp.ones((chunk, chunk), BF16)
    running = jnp.zeros((devices, chunk), F32)
    table = jnp.zeros((devices, 128), F32)
    slots_sub = lax.broadcasted_iota(I32, (128, chunk), 0)
    for i in range(cols // chunk):
        owner = owners_ref[:, pl.ds(i * chunk, chunk)]
        hit = sub == owner
        hot = hit.astype(F32)
        hot16 = hot.astype(BF16)
        earlier = running + jnp.dot(hot16, upper, preferred_element_type=F32)
        slot = jnp.sum(jnp.where(hit, earlier, 0.0), axis=0, keepdims=True).astype(I32)
        running = running + jnp.dot(hot16, ones, preferred_element_type=F32)
        slot_ref[:, pl.ds(i * chunk, chunk)] = slot
        cost = classes_ref[:, pl.ds(i * chunk, chunk)].astype(F32)
        placed = jnp.where(slots_sub == slot, cost, 0.0).astype(BF16)
        table = table + lax.dot_general(
            hot16, placed, (((1,), (1,)), ((), ())), preferred_element_type=F32
        )
    table_ref[...] = table
    copy.wait()

    def element(e, _):
        base = pl.multiple_of(e * 4 * ny, 8)
        for x in range(4):
            nodes_ref[pl.ds(base + x * ny, ny), :] = temper_ref[4 * e + x].astype(F32)
        nodes = [
            [nodes_ref[pl.ds(base + x * ny + k, ne, stride=4), :] for k in range(4)]
            for x in range(4)
        ]
        cells_of(nodes, cells_ref, pl.multiple_of(e * ny, 8), ne)
        return 0

    lax.fori_loop(0, nx // 4, element, 0, unroll=2)
    out_ref[...] = cells_ref[...].astype(BF16)


def columns_stage(owners, classes, temper, devices):
    nx, ny, lev = temper.shape
    cols = owners.shape[1]
    return call(
        columns_kernel,
        [
            jax.ShapeDtypeStruct((1, cols), I32),
            jax.ShapeDtypeStruct((devices, 128), F32),
            jax.ShapeDtypeStruct((cols, lev), BF16),
        ],
        owners, classes, temper,
        vmem=16, flops=10**9, moved=4 * 10**6,
        in_specs=[pl.BlockSpec(memory_space=pltpu.VMEM)] * 2
        + [pl.BlockSpec(memory_space=pltpu.HBM)],
        scratch_shapes=[
            pltpu.VMEM((nx, ny, lev), BF16),
            pltpu.VMEM((nx * ny, lev), F32),
            pltpu.VMEM((nx * ny // 4, lev), F32),
            pltpu.SemaphoreType.DMA,
        ],
    )


CHUNKS = 4


def tendency_kernel(tracer_ref, winds_ref, nodes_ref, tend_ref, u_ref, v_ref):
    nx, ny, lev = tracer_ref.shape
    ne = ny // 4

    def element(e, _):
        base = pl.multiple_of(e * 4 * ny, 8)
        for x in range(4):
            nodes_ref[pl.ds(base + x * ny, ny), :] = tracer_ref[4 * e + x].astype(F32)
            u_ref[pl.ds(base + x * ny, ny), :] = winds_ref[0, 4 * e + x].astype(F32)
            v_ref[pl.ds(base + x * ny, ny), :] = winds_ref[1, 4 * e + x].astype(F32)
        for t in range(ne // 8):
            off = t * 32
            nodes = [
                [nodes_ref[pl.ds(base + x * ny + off + k, 8, stride=4), :] for k in range(4)]
                for x in range(4)
            ]
            for x in range(4):
                for k in range(4):
                    dx = combine(GRAD[x], [nodes[m][k] for m in range(4)])
                    dy = combine(GRAD[k], nodes[x])
                    u = u_ref[pl.ds(base + x * ny + off + k, 8, stride=4), :]
                    v = v_ref[pl.ds(base + x * ny + off + k, 8, stride=4), :]
                    tend_ref[pl.ds(base + x * ny + k * ne + t * 8, 8), :] = -(u * dx + v * dy)
        return 0

    lax.fori_loop(0, nx // 4, element, 0, unroll=2)


def tendency_stage(tracer, winds):
    nx, ny, lev = tracer.shape
    in_vmem = pl.BlockSpec(memory_space=pltpu.VMEM)
    return call(
        tendency_kernel,
        [jax.ShapeDtypeStruct((nx * ny, lev), F32)] * 2,
        tracer, winds,
        vmem=20, flops=2 * 10**9, moved=8 * 10**6,
        in_specs=[in_vmem] * 2,
        out_specs=[in_vmem] * 2,
        scratch_shapes=[pltpu.VMEM((nx * ny, lev), F32)] * 2,
    )


def tracer_kernel(cap, nodes_ref, tend_ref, xprev, xnext, yprev, ynext, owners_ref, slot_ref,
                  table_ref, temper_ref, new_hbm, out_ref, new_ref, fresh_ref, cells_ref,
                  values_ref, low_ref, out_sem):
    nx, ny, lev = new_ref.shape
    ne = ny // 4
    part = nx // CHUNKS
    elements = nx // 4

    def put(c):
        rows = pl.ds(c * part, part)
        return pltpu.make_async_copy(new_ref.at[rows], new_hbm.at[rows], out_sem.at[c])

    first = lax.broadcasted_iota(I32, (ne, lev), 0) == 0
    last = lax.broadcasted_iota(I32, (ne, lev), 0) == ne - 1

    def assemble(e, _):
        base = pl.multiple_of(e * 4 * ny, 8)
        back = pl.multiple_of(jnp.maximum(e * 4 - 1, 0) * ny, 8)
        front = pl.multiple_of(jnp.minimum(e * 4 + 4, nx - 1) * ny, 8)
        rounded = []
        for x in range(4):
            lines = [tend_ref[pl.ds(base + x * ny + k * ne, ne), :] for k in range(4)]
            if x == 0:
                other = [
                    jnp.where(e == 0, xprev[pl.ds(k * ne, ne), :], tend_ref[pl.ds(back + k * ne, ne), :])
                    for k in range(4)
                ]
                lines = [0.5 * (lines[k] + other[k]) for k in range(4)]
            if x == 3:
                other = [
                    jnp.where(
                        e == elements - 1,
                        xnext[pl.ds(k * ne, ne), :],
                        tend_ref[pl.ds(front + k * ne, ne), :],
                    )
                    for k in range(4)
                ]
                lines = [0.5 * (lines[k] + other[k]) for k in range(4)]
            before = yprev[pl.ds(4 * e + x, 1), :]
            after = ynext[pl.ds(4 * e + x, 1), :]
            low = jnp.where(first, before, pltpu.roll(lines[3], 1, 0))
            high = jnp.where(last, after, pltpu.roll(lines[0], ne - 1, 0))
            whole = [0.5 * (lines[0] + low), lines[1], lines[2], 0.5 * (lines[3] + high)]
            row = []
            for k in range(4):
                where = pl.ds(base + x * ny + k, ne, stride=4)
                fresh = (nodes_ref[where, :] + STEP_SIZE * whole[k]).astype(BF16).astype(F32)
                fresh_ref[where, :] = fresh
                row.append(fresh)
            rounded.append(row)
            new_ref[4 * e + x] = fresh_ref[pl.ds(base + x * ny, ny), :].astype(BF16)
        cells_of(rounded, cells_ref, pl.multiple_of(e * ny, 8), ne)
        return 0

    per = part // 4
    for c in range(CHUNKS):
        lax.fori_loop(c * per, (c + 1) * per, assemble, 0, unroll=2)
        put(c).start()
    values_ref[:, :lev] = cells_ref[...].astype(BF16)
    values_ref[:, lev:] = temper_ref[...]
    pack(cap, owners_ref, slot_ref, table_ref, values_ref, low_ref, out_ref)
    for c in range(CHUNKS):
        put(c).wait()


def tracer_stage(shape, nodes, tend, halos, owners, slots, table, temper_cells, cap):
    nx, ny, lev = shape
    cols = owners.shape[1]
    devices = table.shape[0]
    in_vmem = pl.BlockSpec(memory_space=pltpu.VMEM)
    return call(
        functools.partial(tracer_kernel, cap),
        [
            jax.ShapeDtypeStruct((nx, ny, lev), BF16),
            jax.ShapeDtypeStruct((devices * (2 * cap + 8), lev), BF16),
        ],
        nodes, tend, *halos, owners, slots, table, temper_cells,
        vmem=30, flops=4 * 10**9, moved=8 * 10**6,
        in_specs=[in_vmem] * 10,
        out_specs=[pl.BlockSpec(memory_space=pltpu.HBM), in_vmem],
        scratch_shapes=[
            pltpu.VMEM((nx, ny, lev), BF16),
            pltpu.VMEM((nx * ny, lev), F32),
            pltpu.VMEM((cols, lev), F32),
            pltpu.VMEM((cols, 2 * lev), BF16),
            pltpu.VMEM((GROUP * cap, cols), BF16),
            pltpu.SemaphoreType.DMA((CHUNKS,)),
        ],
    )


PIECES = 2


def radiate_kernel(cap, x_ref, aerosol_hbm, win_ref, wout_ref, out_ref, aerosol_ref,
                   depth_a, depth_b, trans_a, trans_b, mask_a, mask_b, sem):
    blocks, rows, width = aerosol_ref.shape
    lev = x_ref.shape[1]
    each = 2 * cap + 8
    sources = rows // cap
    piece = rows // PIECES

    def fetches(block):
        return [
            pltpu.make_async_copy(
                aerosol_hbm.at[pl.ds(block * rows + j * piece, piece)],
                aerosol_ref.at[block, pl.ds(j * piece, piece)],
                sem.at[block, j],
            )
            for j in range(PIECES)
        ]

    for block in range(blocks):
        for copy in fetches(block):
            copy.start()

    lane = lax.broadcasted_iota(I32, (8, lev), 1)
    sub = lax.broadcasted_iota(I32, (8, lev), 0)
    ones = jnp.ones((lev, lev), BF16)

    def begin(block, depth, mask):
        tracer, temper, mine = [], [], []
        for s in range(sources):
            lines = x_ref[pl.ds((block * sources + s) * each, each), :].astype(F32)
            tracer.append(lines[:cap])
            temper.append(lines[cap : 2 * cap])
            mine += [jnp.where(lane == sub + 8 * j, lines[2 * cap :], 0.0) for j in range(cap // 8)]
        state = -jnp.concatenate(
            [jnp.concatenate(tracer, axis=0), jnp.concatenate(temper, axis=0)], axis=1
        ).astype(BF16)
        mine = jnp.concatenate(mine, axis=0).astype(BF16)
        cost = jnp.dot(mine, ones, preferred_element_type=F32)
        for g in range(1, 4):
            mask[g - 1] = (cost > g - 0.5).astype(F32).astype(BF16)
        depth[...] = jnp.dot(state, win_ref[...], preferred_element_type=F32)

    def middle(block, depth, mask, trans):
        step, tile = 256, 64
        parts = width // step
        for i, r in [(i, r) for i in range(parts) for r in range(0, rows, tile)]:
            at, line = pl.ds(i * step, step), pl.ds(r, tile)
            capped = jnp.minimum(depth[line, at], 80.0)
            soft = capped - jnp.log(1.0 + jnp.exp(capped))
            kept = jnp.exp(soft * aerosol_ref[block, line, at].astype(F32)).astype(BF16)
            group = i * 4 // parts
            if group:
                kept = kept * jnp.concatenate([mask[group - 1, line]] * (step // lev), axis=1)
            trans[line, at] = kept

    def finish(block, trans):
        out_ref[pl.ds(block * rows, rows), :] = jnp.dot(
            trans[...], wout_ref[...], preferred_element_type=F32
        ).astype(BF16)

    begin(0, depth_a, mask_a)

    def pair(i, _):
        first = 2 * i
        for copy in fetches(first) + fetches(first + 1):
            copy.wait()
        begin(first + 1, depth_b, mask_b)
        finish(jnp.maximum(first - 1, 0), trans_b)
        middle(first, depth_a, mask_a, trans_a)
        begin(jnp.minimum(first + 2, blocks - 1), depth_a, mask_a)
        finish(first, trans_a)
        middle(first + 1, depth_b, mask_b, trans_b)
        return 0

    lax.fori_loop(0, blocks // 2, pair, 0)
    finish(blocks - 1, trans_b)


def radiate(arrived, aerosol, band_in, band_out, cap):
    lev = arrived.shape[1]
    rows, width = aerosol.shape
    block = 16 * cap
    in_vmem = pl.BlockSpec(memory_space=pltpu.VMEM)
    return call(
        functools.partial(radiate_kernel, cap),
        jax.ShapeDtypeStruct((rows, 2 * lev), BF16),
        arrived, aerosol, band_in, band_out,
        vmem=46, flops=7 * 10**9, moved=20 * 10**6,
        in_specs=[in_vmem, pl.BlockSpec(memory_space=pltpu.HBM), in_vmem, in_vmem],
        scratch_shapes=[
            pltpu.VMEM((rows // block, block, width), BF16),
            pltpu.VMEM((block, width), F32),
            pltpu.VMEM((block, width), F32),
            pltpu.VMEM((block, width), BF16),
            pltpu.VMEM((block, width), BF16),
            pltpu.VMEM((3, block, lev), BF16),
            pltpu.VMEM((3, block, lev), BF16),
            pltpu.SemaphoreType.DMA((rows // block, PIECES)),
        ],
    )


def gather_kernel(cap, owners_ref, slot_ref, back_ref, out_hbm, out_ref, hot_ref, sem):
    cols, rows = out_ref.shape[0], back_ref.shape[0]
    block, wide = hot_ref.shape[1], 128
    lane = lax.broadcasted_iota(I32, (wide, wide), 1)
    none = jnp.zeros((wide, wide), BF16)

    def ship(i):
        at = pl.ds(i * block, block)
        return pltpu.make_async_copy(out_ref.at[at], out_hbm.at[at], sem.at[i])

    for i in range(cols // block):
        for j in range(block // wide):
            at = pl.ds(i * block + j * wide, wide)
            line = (owners_ref[:, at] * cap + slot_ref[:, at]).astype(F32)
            place = jnp.transpose(jnp.broadcast_to(line, (wide, wide))).astype(I32)
            high = (place >> 7).astype(F32).astype(BF16)
            low = (lane == (place & (wide - 1))).astype(F32).astype(BF16)
            for r in range(rows // wide):
                here = jnp.full((wide, wide), float(r), BF16)
                hot_ref[i % 2, pl.ds(j * wide, wide), pl.ds(r * wide, wide)] = jnp.where(
                    high == here, low, none
                )
        out_ref[pl.ds(i * block, block), :] = jnp.dot(
            hot_ref[i % 2], back_ref[...], preferred_element_type=F32
        ).astype(BF16)
        ship(i).start()
    for i in range(cols // block):
        ship(i).wait()


def gather(owners, slots, back, cap):
    return call(
        functools.partial(gather_kernel, cap),
        jax.ShapeDtypeStruct((owners.shape[1], back.shape[1]), BF16),
        owners, slots, back,
        vmem=24, flops=3 * 10**9, moved=3 * 10**6,
        in_specs=[pl.BlockSpec(memory_space=pltpu.VMEM)] * 3,
        out_specs=pl.BlockSpec(memory_space=pl.ANY),
        scratch_shapes=[
            pltpu.VMEM((owners.shape[1], back.shape[1]), BF16),
            pltpu.VMEM((2, owners.shape[1] // 4, back.shape[0]), BF16),
            pltpu.SemaphoreType.DMA((4,)),
        ],
    )


def exchange(x):
    return lax.all_to_all(x, ("dyn", "col"), split_axis=0, concat_axis=0, tiled=True)


def shards(tracer, temper, winds, owners, classes, aerosol, band_in, band_out):
    n_dyn, n_col = lax.axis_size("dyn"), lax.axis_size("col")
    devices = n_dyn * n_col
    lev = tracer.shape[2]
    cap = aerosol.shape[1] // devices

    def send(x, by_dyn, by_col):
        pairs = [
            (i * n_col + j, ((i + by_dyn) % n_dyn) * n_col + (j + by_col) % n_col)
            for i in range(n_dyn)
            for j in range(n_col)
        ]
        return lax.ppermute(x, ("dyn", "col"), pairs)

    owners = owners.reshape(1, -1)
    ex0, ex3, ey0, ey3 = edges(tracer, winds)
    xprev, xnext = send(ex3, 1, 0), send(ex0, -1, 0)
    nodes, tend = tendency_stage(tracer, winds)
    slots, table, temper_cells = columns_stage(owners, classes.reshape(1, -1), temper, devices)
    side0, side3 = sides(ey0, ey3, xprev, xnext)
    yprev, ynext = send(side3, 0, 1), send(side0, 0, -1)
    tracer_new, outgoing = tracer_stage(
        tracer.shape, nodes, tend, (xprev, xnext, yprev, ynext), owners, slots, table, temper_cells, cap
    )
    each = 2 * cap + 8
    arrived = exchange(outgoing.reshape(devices, each, lev)).reshape(-1, lev)
    result = radiate(arrived, aerosol[0], band_in, band_out, cap)
    back = exchange(result.reshape(devices, cap, 2 * lev)).reshape(-1, 2 * lev)
    return (tracer_new, gather(owners, slots, back, cap))


def solution(mesh):
    return jax.shard_map(
        shards,
        mesh=mesh,
        in_specs=(
            P("dyn", "col", None),
            P("dyn", "col", None),
            P(None, "dyn", "col", None),
            P(("dyn", "col"), None),
            P(("dyn", "col")),
            P(("dyn", "col"), None, None),
            P(),
            P(),
        ),
        out_specs=(P("dyn", "col", None), P(("dyn", "col"), None)),
        check_vma=False,
    )
```

time: 217 us -> 106 us (0.49)
  blocking collectives: 0 us -> 65.4 us
  local copies, waits for them, and re-layouts: 61.9 us -> 0.04 us
  waiting for transfers between devices: 47.4 us -> 1.82 us
  matrix products: 40.3 us -> 0 us
  other arithmetic: 36 us -> 0 us
  Pallas kernels: 0 us -> 29 us
  starting transfers between devices: 29.6 us -> 8.46 us
    all_to_all x0 -> x2, blocking collectives: none -> 65.4 us  [exchange(): lax.all_to_all(x, ('dyn', 'col'), split_axis=0, concat_axis=0, tiled=True)]
    all_to_all x3 -> x0, waiting for transfers between devices: 43.9 us -> none  [the longest x1 22.6 us: shards(): lax.all_to_all(result.reshape(devices, capacity, width_two), ('dyn', 'col...]
    dot_general x12 -> x0, matrix products: 40.3 us -> none  [the longest x6 31.5 us: radiate(): optical_depth = jnp.dot(state, band_in, preferred_element_type=jnp.float32)]
    pallas_call x0 -> x7, Pallas kernels: none -> 29 us  [call(): pl.pallas_call(kernel, out_shape=out_shape, compiler_params=pltpu.Compile...]
    dynamic_slice x12 -> x0, local copies, waits for them, and re-layouts: 25.6 us -> none  [radiate_blocks(): lax.map(one_block, (state.reshape(count, block, -1), cost_class.reshape(c...]
    all_to_all x3 -> x0, starting transfers between devices: 21.7 us -> none  [the longest x1 8.75 us: shards(): lax.all_to_all(outgoing.reshape(devices, capacity, width_two), ('dyn', 'c...]
    scatter x1 -> x0, local copies, waits for them, and re-layouts: 11.1 us -> none  [shards(): jnp.zeros((devices * capacity,), jnp.bfloat16).at[target]]
    add x5 -> x0, other arithmetic: 10.3 us -> none  [apply_small(): total = term if total is None else total + term]
  transfers between devices with their start and end apart: 7 -> 4, of which waited for: 4 -> 1; matrix products, arithmetic and copies ran while one was open for 17% -> 0% of each run, Pallas kernels for 0% -> 3%
where the time goes in v1:
time: 106 us
  blocking collectives  65.4 us (62%)
  Pallas kernels  29 us (27%)
  starting transfers between devices  8.46 us (8%)
  waiting for transfers between devices  1.82 us (2%)
    all_to_all x2, blocking collectives, exchange(): lax.all_to_all(x, ('dyn', 'col'), split_axis=0, concat_axis=0, tiled=True)  65.4 us
    pallas_call x7, Pallas kernels, call(): pl.pallas_call(kernel, out_shape=out_shape, compiler_params=pltpu.Compile...  29 us
    ppermute x4, starting transfers between devices, send(): return lax.ppermute(x, ('dyn', 'col'), pairs)  8.46 us
  transfers between devices with their start and end apart: 4, of which 1 were waited for; matrix products, arithmetic and copies ran while one was open for 0% of the time, Pallas kernels for 3%

profile of v1, /device:TPU:1, one launch (start us, length us, event | category | flops | bytes accessed | tf_op | source)
XLA Modules:
  0.0 105.6 jit_solution(1809940681205621140)
XLA Ops:
  0.6 0.0 copy-start
  0.6 0.0 copy-start.1
  0.6 1.9 %shard_map.96 = (f32[96,128]{1,0:T(8,128)S(1)}, f32[96,128]{1,0:T(8,128)S(1)}, f32[64,128]{1,0:T(8,128)S(1)}, f32[64,128]{1,0:T(8,128)S(1)}) custom-call(bf16[64,96,128]{2,1,0:T(8,128)(2,1)} %tracer.1, bf16[2,64,96,128]{3,2,1,0:T(8,128)(2,1)} %winds.1), custom_call_target="tpu_custom_call" | custom-call | flops 1000000 | bytes 3000000 | tf_op jit(solution)/shard_map/pallas_call | solution.py:53
  2.6 2.1 %collective-permute-start = (f32[96,128]{1,0:T(8,128)S(1)}, f32[96,128]{1,0:T(8,128)S(1)}, u32[]{:S(2)}, u32[]{:S(2)}) collective-permute-start(f32[96,128]{1,0:T(8,128)S(1)} %get-tuple-element.17), channel_id=1, source_target_pairs={{0,8},{1,9},{2,10},{3,11},{4,12},{5,13},{6,14},{7,15},{8,16},{9,17... | collective-permute-start | bytes 147464 | tf_op jit(solution)/shard_map/ppermute | solution.py:576
  4.7 0.0 copy-start.6
  4.7 0.0 copy-start.2
  4.7 0.0 copy-start.5
  4.7 3.8 %collective-permute-start.1 = (f32[96,128]{1,0:T(8,128)S(1)}, f32[96,128]{1,0:T(8,128)S(1)}, u32[]{:S(2)}, u32[]{:S(2)}) collective-permute-start(f32[96,128]{1,0:T(8,128)S(1)} %get-tuple-element.18), channel_id=1, source_target_pairs={{0,120},{1,121},{2,122},{3,123},{4,124},{5,125},{6,126},{7,127},{8... | collective-permute-start | bytes 147464 | tf_op jit(solution)/shard_map/ppermute | solution.py:576
  8.5 0.0 copy-done
  8.5 0.0 copy-done.1
  8.5 2.1 %shard_map.95 = (f32[6144,128]{1,0:T(8,128)S(1)}, f32[6144,128]{1,0:T(8,128)S(1)}) custom-call(bf16[64,96,128]{2,1,0:T(8,128)(2,1)S(1)} %copy-done.1, bf16[2,64,96,128]{3,2,1,0:T(8,128)(2,1)S(1)} %copy-done), custom_call_target="tpu_custom_call" | custom-call | flops 2000000000 | bytes 8000000 | tf_op jit(solution)/shard_map/pallas_call | solution.py:53
  10.7 0.0 copy-done.6
  10.7 0.0 collective-permute-done.xprev
  10.7 0.0 collective-permute-done.1.xnext
  10.7 2.5 %collective-permute-start.2 = (f32[64,128]{1,0:T(8,128)S(1)}, f32[64,128]{1,0:T(8,128)S(1)}, u32[]{:S(2)}, u32[]{:S(2)}) collective-permute-start(f32[64,128]{1,0:T(8,128)S(1)} %get-tuple-element.21), channel_id=1, source_target_pairs={{0,1},{1,2},{2,3},{3,4},{4,5},{5,6},{6,7},{7,0},{8,9},{9,10},{10,1... | collective-permute-start | bytes 98312 | tf_op jit(solution)/shard_map/ppermute | solution.py:576
  13.3 0.0 collective-permute-start.3
  13.3 0.0 copy-done.2
  13.3 0.0 copy-done.5
  13.3 1.5 %shard_map.98 = (s32[1,1536]{1,0:T(1,128)S(1)}, f32[128,128]{1,0:T(8,128)S(1)}, bf16[1536,128]{1,0:T(8,128)(2,1)S(1)}) custom-call(s32[1,1536]{1,0:T(1,128)S(1)} %bitcast.10, s32[1,1536]{1,0:T(1,128)S(1)} %reshape.23.classes_ref, bf16[64,96,128]{2,1,0:T(8,128)(2,1)S(1)} %copy-done.2), custom_call_target="tpu_custom_call" | custom-call | flops 1000000000 | bytes 4000000 | tf_op jit(solution)/shard_map/pallas_call | solution.py:53
  14.8 0.0 collective-permute-done.2.yprev
  14.8 1.8 %collective-permute-done.3.ynext = f32[64,128]{1,0:T(8,128)S(1)} collective-permute-done((f32[64,128]{1,0:T(8,128)S(1)}, f32[64,128]{1,0:T(8,128)S(1)}, u32[]{:S(2)}, u32[]{:S(2)}) %collective-permute-start.3) | collective-permute-done | bytes 32800 | tf_op jit(solution)/shard_map/ppermute | solution.py:576
  16.6 4.1 %shard_map.99 = (bf16[64,96,128]{2,1,0:T(8,128)(2,1)}, bf16[7168,128]{1,0:T(8,128)(2,1)S(1)}) custom-call(f32[6144,128]{1,0:T(8,128)S(1)} %get-tuple-element.15.nodes_ref, f32[6144,128]{1,0:T(8,128)S(1)} %get-tuple-element.16.tend_ref, f32[96,128]{1,0:T(8,128)S(1)} %collective-permute-done.xprev, f32[96,128]{1,0:T(8,128)S(1)} %collective-permute-done.1.xnext, ...), custom_call_target="tpu_custom_call" | custom-call | flops 4000000000 | bytes 8000000 | tf_op jit(solution)/shard_map/pallas_call | solution.py:53
  20.7 0.0 copy-start.3
  20.7 0.0 copy-start.4
  20.7 36.5 %all_to_all.10 = bf16[128,56,128]{2,1,0:T(8,128)(2,1)S(1)} all-to-all(bf16[128,56,128]{2,1,0:T(8,128)(2,1)S(1)} %bitcast.6), channel_id=1, replica_groups=mesh['dyn'=16,'col'=8] {'dyn','col'}, dimensions={0} | all-to-all | bytes 3670016 | tf_op jit(solution)/shard_map/all_to_all | solution.py:561
  57.2 0.0 copy-done.3
  57.2 0.0 copy-done.4
  57.2 15.6 %shard_map.100 = bf16[3072,256]{1,0:T(8,128)(2,1)S(1)} custom-call(bf16[7168,128]{1,0:T(8,128)(2,1)S(1)} %bitcast.7, bf16[3072,2048]{1,0:T(8,128)(2,1)} %bitcast.13, bf16[256,2048]{1,0:T(8,128)(2,1)S(1)} %copy-done.3, bf16[2048,256]{1,0:T(8,128)(2,1)S(1)} %copy-done.4), custom_call_target="tpu_custom_call" | custom-call | flops 7000000000 | bytes 20000000 | tf_op jit(solution)/shard_map/pallas_call | solution.py:53
  72.9 28.9 %all_to_all.11 = bf16[128,24,256]{2,1,0:T(8,128)(2,1)S(1)} all-to-all(bf16[128,24,256]{2,1,0:T(8,128)(2,1)S(1)} %bitcast.9), channel_id=1, replica_groups=mesh['dyn'=16,'col'=8] {'dyn','col'}, dimensions={0} | all-to-all | bytes 3145728 | tf_op jit(solution)/shard_map/all_to_all | solution.py:561
  101.7 3.7 %shard_map.101 = bf16[1536,256]{1,0:T(8,128)(2,1)} custom-call(s32[1,1536]{1,0:T(1,128)S(1)} %bitcast.12, s32[1,1536]{1,0:T(1,128)S(1)} %get-tuple-element.23.slot_ref, bf16[3072,256]{1,0:T(8,128)(2,1)S(1)} %bitcast.8), custom_call_target="tpu_custom_call" | custom-call | flops 3000000000 | bytes 3000000 | tf_op jit(solution)/shard_map/pallas_call | solution.py:53
  (2 shorter events, 0.0 us)
Async XLA Ops:
  0.6 7.9 %copy-start = (bf16[2,64,96,128]{3,2,1,0:T(8,128)(2,1)S(1)}, bf16[2,64,96,128]{3,2,1,0:T(8,128)(2,1)}, u32[]{:S(2)}) copy-start(bf16[2,64,96,128]{3,2,1,0:T(8,128)(2,1)} %winds.1) | copy-start | bytes 9437188
  0.6 7.9 %copy-start.1 = (bf16[64,96,128]{2,1,0:T(8,128)(2,1)S(1)}, bf16[64,96,128]{2,1,0:T(8,128)(2,1)}, u32[]{:S(2)}) copy-start(bf16[64,96,128]{2,1,0:T(8,128)(2,1)} %tracer.1) | copy-start | bytes 4718596
  2.6 8.1 %collective-permute-start = (f32[96,128]{1,0:T(8,128)S(1)}, f32[96,128]{1,0:T(8,128)S(1)}, u32[]{:S(2)}, u32[]{:S(2)}) collective-permute-start(f32[96,128]{1,0:T(8,128)S(1)} %get-tuple-element.17), channel_id=1, source_target_pairs={{0,8},{1,9},{2,10},{3,11},{4,12},{5,13},{6,14},{7,15},{8,16},{9,17... | collective-permute-start | bytes 147464 | tf_op jit(solution)/shard_map/ppermute | solution.py:576
  4.7 6.0 %copy-start.6 = (s32[1536]{0:T(1024)S(1)}, s32[1536]{0:T(1024)}, u32[]{:S(2)}) copy-start(s32[1536]{0:T(1024)} %param.12) | copy-start | bytes 18436
  4.7 8.6 %copy-start.2 = (bf16[64,96,128]{2,1,0:T(8,128)(2,1)S(1)}, bf16[64,96,128]{2,1,0:T(8,128)(2,1)}, u32[]{:S(2)}) copy-start(bf16[64,96,128]{2,1,0:T(8,128)(2,1)} %temper_hbm.1) | copy-start | bytes 4718596
  4.7 8.6 %copy-start.5 = (s32[1536,1]{0,1:T(1,128)S(1)}, s32[1536,1]{0,1:T(1,128)}, u32[]{:S(2)}) copy-start(s32[1536,1]{0,1:T(1,128)} %param.11) | copy-start | bytes 18436
  4.7 6.0 %collective-permute-start.1 = (f32[96,128]{1,0:T(8,128)S(1)}, f32[96,128]{1,0:T(8,128)S(1)}, u32[]{:S(2)}, u32[]{:S(2)}) collective-permute-start(f32[96,128]{1,0:T(8,128)S(1)} %get-tuple-element.18), channel_id=1, source_target_pairs={{0,120},{1,121},{2,122},{3,123},{4,124},{5,125},{6,126},{7,127},{8... | collective-permute-start | bytes 147464 | tf_op jit(solution)/shard_map/ppermute | solution.py:576
  10.7 4.0 %collective-permute-start.2 = (f32[64,128]{1,0:T(8,128)S(1)}, f32[64,128]{1,0:T(8,128)S(1)}, u32[]{:S(2)}, u32[]{:S(2)}) collective-permute-start(f32[64,128]{1,0:T(8,128)S(1)} %get-tuple-element.21), channel_id=1, source_target_pairs={{0,1},{1,2},{2,3},{3,4},{4,5},{5,6},{6,7},{7,0},{8,9},{9,10},{10,1... | collective-permute-start | bytes 98312 | tf_op jit(solution)/shard_map/ppermute | solution.py:576
  13.3 3.3 %collective-permute-start.3 = (f32[64,128]{1,0:T(8,128)S(1)}, f32[64,128]{1,0:T(8,128)S(1)}, u32[]{:S(2)}, u32[]{:S(2)}) collective-permute-start(f32[64,128]{1,0:T(8,128)S(1)} %get-tuple-element.22), channel_id=1, source_target_pairs={{0,7},{1,0},{2,1},{3,2},{4,3},{5,4},{6,5},{7,6},{8,15},{9,8},{10,9... | collective-permute-start | bytes 98312 | tf_op jit(solution)/shard_map/ppermute | solution.py:576
  20.7 36.6 %copy-start.3 = (bf16[256,2048]{1,0:T(8,128)(2,1)S(1)}, bf16[256,2048]{1,0:T(8,128)(2,1)}, u32[]{:S(2)}) copy-start(bf16[256,2048]{1,0:T(8,128)(2,1)} %win_ref.1) | copy-start | bytes 3145732
  20.7 36.5 %copy-start.4 = (bf16[2048,256]{1,0:T(8,128)(2,1)S(1)}, bf16[2048,256]{1,0:T(8,128)(2,1)}, u32[]{:S(2)}) copy-start(bf16[2048,256]{1,0:T(8,128)(2,1)} %wout_ref.1) | copy-start | bytes 3145732

commit v2 on v1

--- a/solution.py
+++ b/solution.py
@@ -12,6 +12,7 @@
 STEP_SIZE = 0.1
 F32, BF16, I32 = jnp.float32, jnp.bfloat16, jnp.int32
 MIB = 1024 * 1024
+LOG2E = 1.4426950408889634
 
 
 def lagrange_tables():
@@ -46,7 +47,7 @@
 
 def cell_pair(nodes):
     halves = [[combine(PG2[a], [nodes[x][k] for x in range(4)]) for k in range(4)] for a in range(2)]
-    return [[combine(PG2[b], halves[a]) for b in range(2)] for a in range(2)]
+    return [[combine(-LOG2E * PG2[b], halves[a]) for b in range(2)] for a in range(2)]
 
 
 def call(kernel, out_shape, *args, vmem, flops=0, moved=0, **kw):
@@ -410,7 +411,7 @@
 
 
 def radiate_kernel(cap, x_ref, aerosol_hbm, win_ref, wout_ref, out_ref, aerosol_ref,
-                   depth_a, depth_b, trans_a, trans_b, mask_a, mask_b, sem):
+                   depth_a, depth_b, trans_a, trans_b, bound_a, bound_b, sem):
     blocks, rows, width = aerosol_ref.shape
     lev = x_ref.shape[1]
     each = 2 * cap + 8
@@ -435,33 +436,32 @@
     sub = lax.broadcasted_iota(I32, (8, lev), 0)
     ones = jnp.ones((lev, lev), BF16)
 
-    def begin(block, depth, mask):
+    def begin(block, depth, bound):
         tracer, temper, mine = [], [], []
         for s in range(sources):
             lines = x_ref[pl.ds((block * sources + s) * each, each), :].astype(F32)
             tracer.append(lines[:cap])
             temper.append(lines[cap : 2 * cap])
             mine += [jnp.where(lane == sub + 8 * j, lines[2 * cap :], 0.0) for j in range(cap // 8)]
-        state = -jnp.concatenate(
+        state = jnp.concatenate(
             [jnp.concatenate(tracer, axis=0), jnp.concatenate(temper, axis=0)], axis=1
         ).astype(BF16)
         mine = jnp.concatenate(mine, axis=0).astype(BF16)
         cost = jnp.dot(mine, ones, preferred_element_type=F32)
         for g in range(1, 4):
-            mask[g - 1] = (cost > g - 0.5).astype(F32).astype(BF16)
+            bound[g - 1] = jnp.where(cost > g - 0.5, 120.0, -1e30)
         depth[...] = jnp.dot(state, win_ref[...], preferred_element_type=F32)
 
-    def middle(block, depth, mask, trans):
+    def middle(block, depth, bound, trans):
         step, tile = 256, 64
         parts = width // step
         for i, r in [(i, r) for i in range(parts) for r in range(0, rows, tile)]:
             at, line = pl.ds(i * step, step), pl.ds(r, tile)
-            capped = jnp.minimum(depth[line, at], 80.0)
-            soft = capped - jnp.log(1.0 + jnp.exp(capped))
-            kept = jnp.exp(soft * aerosol_ref[block, line, at].astype(F32)).astype(BF16)
             group = i * 4 // parts
-            if group:
-                kept = kept * jnp.concatenate([mask[group - 1, line]] * (step // lev), axis=1)
+            top = jnp.concatenate([bound[group - 1, line]] * (step // lev), axis=1) if group else 120.0
+            capped = jnp.minimum(depth[line, at], top)
+            soft = capped - jnp.log2(1.0 + jnp.exp2(capped))
+            kept = jnp.exp2(soft * aerosol_ref[block, line, at].astype(F32)).astype(BF16)
             trans[line, at] = kept
 
     def finish(block, trans):
@@ -469,18 +469,20 @@
             trans[...], wout_ref[...], preferred_element_type=F32
         ).astype(BF16)
 
-    begin(0, depth_a, mask_a)
+    begin(0, depth_a, bound_a)
 
     def pair(i, _):
         first = 2 * i
-        for copy in fetches(first) + fetches(first + 1):
+        for copy in fetches(first):
             copy.wait()
-        begin(first + 1, depth_b, mask_b)
+        begin(first + 1, depth_b, bound_b)
         finish(jnp.maximum(first - 1, 0), trans_b)
-        middle(first, depth_a, mask_a, trans_a)
-        begin(jnp.minimum(first + 2, blocks - 1), depth_a, mask_a)
+        middle(first, depth_a, bound_a, trans_a)
+        for copy in fetches(first + 1):
+            copy.wait()
+        begin(jnp.minimum(first + 2, blocks - 1), depth_a, bound_a)
         finish(first, trans_a)
-        middle(first + 1, depth_b, mask_b, trans_b)
+        middle(first + 1, depth_b, bound_b, trans_b)
         return 0
 
     lax.fori_loop(0, blocks // 2, pair, 0)
@@ -504,8 +506,8 @@
             pltpu.VMEM((block, width), F32),
             pltpu.VMEM((block, width), BF16),
             pltpu.VMEM((block, width), BF16),
-            pltpu.VMEM((3, block, lev), BF16),
-            pltpu.VMEM((3, block, lev), BF16),
+            pltpu.VMEM((3, block, lev), F32),
+            pltpu.VMEM((3, block, lev), F32),
             pltpu.SemaphoreType.DMA((rows // block, PIECES)),
         ],
     )

time: 106 us -> 103 us (0.972)
  Pallas kernels: 29 us -> 26.2 us
    pallas_call x7, Pallas kernels: 29 us -> 26.2 us  [call(): pl.pallas_call(kernel, out_shape=out_shape, compiler_params=pltpu.Compile...]
  transfers between devices with their start and end apart: 4 -> 4, of which waited for: 1 -> 1; matrix products, arithmetic and copies ran while one was open for 0% -> 0% of each run, Pallas kernels for 3% -> 4%
where the time goes in v2:
time: 103 us
  blocking collectives  65.4 us (63%)
  Pallas kernels  26.2 us (25%)
  starting transfers between devices  8.46 us (8%)
  waiting for transfers between devices  1.82 us (2%)
    all_to_all x2, blocking collectives, exchange(): lax.all_to_all(x, ('dyn', 'col'), split_axis=0, concat_axis=0, tiled=True)  65.4 us
    pallas_call x7, Pallas kernels, call(): pl.pallas_call(kernel, out_shape=out_shape, compiler_params=pltpu.Compile...  26.2 us
    ppermute x4, starting transfers between devices, send(): return lax.ppermute(x, ('dyn', 'col'), pairs)  8.46 us
  transfers between devices with their start and end apart: 4, of which 1 were waited for; matrix products, arithmetic and copies ran while one was open for 0% of the time, Pallas kernels for 4%

profile of v2, /device:TPU:1, one launch (start us, length us, event | category | flops | bytes accessed | tf_op | source)
XLA Modules:
  0.0 102.8 jit_solution(17429651285199964905)
XLA Ops:
  0.6 0.0 copy-start
  0.6 0.0 copy-start.1
  0.6 1.9 %shard_map.96 = (f32[96,128]{1,0:T(8,128)S(1)}, f32[96,128]{1,0:T(8,128)S(1)}, f32[64,128]{1,0:T(8,128)S(1)}, f32[64,128]{1,0:T(8,128)S(1)}) custom-call(bf16[64,96,128]{2,1,0:T(8,128)(2,1)} %tracer.1, bf16[2,64,96,128]{3,2,1,0:T(8,128)(2,1)} %winds.1), custom_call_target="tpu_custom_call" | custom-call | flops 1000000 | bytes 3000000 | tf_op jit(solution)/shard_map/pallas_call | solution.py:54
  2.6 2.1 %collective-permute-start = (f32[96,128]{1,0:T(8,128)S(1)}, f32[96,128]{1,0:T(8,128)S(1)}, u32[]{:S(2)}, u32[]{:S(2)}) collective-permute-start(f32[96,128]{1,0:T(8,128)S(1)} %get-tuple-element.17), channel_id=1, source_target_pairs={{0,8},{1,9},{2,10},{3,11},{4,12},{5,13},{6,14},{7,15},{8,16},{9,17... | collective-permute-start | bytes 147464 | tf_op jit(solution)/shard_map/ppermute | solution.py:578
  4.7 0.0 copy-start.6
  4.7 0.0 copy-start.2
  4.7 0.0 copy-start.5
  4.7 3.8 %collective-permute-start.1 = (f32[96,128]{1,0:T(8,128)S(1)}, f32[96,128]{1,0:T(8,128)S(1)}, u32[]{:S(2)}, u32[]{:S(2)}) collective-permute-start(f32[96,128]{1,0:T(8,128)S(1)} %get-tuple-element.18), channel_id=1, source_target_pairs={{0,120},{1,121},{2,122},{3,123},{4,124},{5,125},{6,126},{7,127},{8... | collective-permute-start | bytes 147464 | tf_op jit(solution)/shard_map/ppermute | solution.py:578
  8.5 0.0 copy-done
  8.5 0.0 copy-done.1
  8.5 2.1 %shard_map.95 = (f32[6144,128]{1,0:T(8,128)S(1)}, f32[6144,128]{1,0:T(8,128)S(1)}) custom-call(bf16[64,96,128]{2,1,0:T(8,128)(2,1)S(1)} %copy-done.1, bf16[2,64,96,128]{3,2,1,0:T(8,128)(2,1)S(1)} %copy-done), custom_call_target="tpu_custom_call" | custom-call | flops 2000000000 | bytes 8000000 | tf_op jit(solution)/shard_map/pallas_call | solution.py:54
  10.7 0.0 copy-done.6
  10.7 0.0 collective-permute-done.xprev
  10.7 0.0 collective-permute-done.1.xnext
  10.7 2.5 %collective-permute-start.2 = (f32[64,128]{1,0:T(8,128)S(1)}, f32[64,128]{1,0:T(8,128)S(1)}, u32[]{:S(2)}, u32[]{:S(2)}) collective-permute-start(f32[64,128]{1,0:T(8,128)S(1)} %get-tuple-element.21), channel_id=1, source_target_pairs={{0,1},{1,2},{2,3},{3,4},{4,5},{5,6},{6,7},{7,0},{8,9},{9,10},{10,1... | collective-permute-start | bytes 98312 | tf_op jit(solution)/shard_map/ppermute | solution.py:578
  13.3 0.0 collective-permute-start.3
  13.3 0.0 copy-done.2
  13.3 0.0 copy-done.5
  13.3 1.5 %shard_map.98 = (s32[1,1536]{1,0:T(1,128)S(1)}, f32[128,128]{1,0:T(8,128)S(1)}, bf16[1536,128]{1,0:T(8,128)(2,1)S(1)}) custom-call(s32[1,1536]{1,0:T(1,128)S(1)} %bitcast.10, s32[1,1536]{1,0:T(1,128)S(1)} %reshape.23.classes_ref, bf16[64,96,128]{2,1,0:T(8,128)(2,1)S(1)} %copy-done.2), custom_call_target="tpu_custom_call" | custom-call | flops 1000000000 | bytes 4000000 | tf_op jit(solution)/shard_map/pallas_call | solution.py:54
  14.8 0.0 collective-permute-done.2.yprev
  14.8 1.8 %collective-permute-done.3.ynext = f32[64,128]{1,0:T(8,128)S(1)} collective-permute-done((f32[64,128]{1,0:T(8,128)S(1)}, f32[64,128]{1,0:T(8,128)S(1)}, u32[]{:S(2)}, u32[]{:S(2)}) %collective-permute-start.3) | collective-permute-done | bytes 32800 | tf_op jit(solution)/shard_map/ppermute | solution.py:578
  16.6 4.1 %shard_map.99 = (bf16[64,96,128]{2,1,0:T(8,128)(2,1)}, bf16[7168,128]{1,0:T(8,128)(2,1)S(1)}) custom-call(f32[6144,128]{1,0:T(8,128)S(1)} %get-tuple-element.15.nodes_ref, f32[6144,128]{1,0:T(8,128)S(1)} %get-tuple-element.16.tend_ref, f32[96,128]{1,0:T(8,128)S(1)} %collective-permute-done.xprev, f32[96,128]{1,0:T(8,128)S(1)} %collective-permute-done.1.xnext, ...), custom_call_target="tpu_custom_call" | custom-call | flops 4000000000 | bytes 8000000 | tf_op jit(solution)/shard_map/pallas_call | solution.py:54
  20.7 0.0 copy-start.3
  20.7 0.0 copy-start.4
  20.7 36.5 %all_to_all.10 = bf16[128,56,128]{2,1,0:T(8,128)(2,1)S(1)} all-to-all(bf16[128,56,128]{2,1,0:T(8,128)(2,1)S(1)} %bitcast.6), channel_id=1, replica_groups=mesh['dyn'=16,'col'=8] {'dyn','col'}, dimensions={0} | all-to-all | bytes 3670016 | tf_op jit(solution)/shard_map/all_to_all | solution.py:563
  57.2 0.0 copy-done.3
  57.2 0.0 copy-done.4
  57.2 12.8 %shard_map.100 = bf16[3072,256]{1,0:T(8,128)(2,1)S(1)} custom-call(bf16[7168,128]{1,0:T(8,128)(2,1)S(1)} %bitcast.7, bf16[3072,2048]{1,0:T(8,128)(2,1)} %bitcast.13, bf16[256,2048]{1,0:T(8,128)(2,1)S(1)} %copy-done.3, bf16[2048,256]{1,0:T(8,128)(2,1)S(1)} %copy-done.4), custom_call_target="tpu_custom_call" | custom-call | flops 7000000000 | bytes 20000000 | tf_op jit(solution)/shard_map/pallas_call | solution.py:54
  70.1 28.9 %all_to_all.11 = bf16[128,24,256]{2,1,0:T(8,128)(2,1)S(1)} all-to-all(bf16[128,24,256]{2,1,0:T(8,128)(2,1)S(1)} %bitcast.9), channel_id=1, replica_groups=mesh['dyn'=16,'col'=8] {'dyn','col'}, dimensions={0} | all-to-all | bytes 3145728 | tf_op jit(solution)/shard_map/all_to_all | solution.py:563
  98.9 3.7 %shard_map.101 = bf16[1536,256]{1,0:T(8,128)(2,1)} custom-call(s32[1,1536]{1,0:T(1,128)S(1)} %bitcast.12, s32[1,1536]{1,0:T(1,128)S(1)} %get-tuple-element.23.slot_ref, bf16[3072,256]{1,0:T(8,128)(2,1)S(1)} %bitcast.8), custom_call_target="tpu_custom_call" | custom-call | flops 3000000000 | bytes 3000000 | tf_op jit(solution)/shard_map/pallas_call | solution.py:54
  (2 shorter events, 0.0 us)
Async XLA Ops:
  0.6 7.9 %copy-start = (bf16[2,64,96,128]{3,2,1,0:T(8,128)(2,1)S(1)}, bf16[2,64,96,128]{3,2,1,0:T(8,128)(2,1)}, u32[]{:S(2)}) copy-start(bf16[2,64,96,128]{3,2,1,0:T(8,128)(2,1)} %winds.1) | copy-start | bytes 9437188
  0.6 7.9 %copy-start.1 = (bf16[64,96,128]{2,1,0:T(8,128)(2,1)S(1)}, bf16[64,96,128]{2,1,0:T(8,128)(2,1)}, u32[]{:S(2)}) copy-start(bf16[64,96,128]{2,1,0:T(8,128)(2,1)} %tracer.1) | copy-start | bytes 4718596
  2.6 8.1 %collective-permute-start = (f32[96,128]{1,0:T(8,128)S(1)}, f32[96,128]{1,0:T(8,128)S(1)}, u32[]{:S(2)}, u32[]{:S(2)}) collective-permute-start(f32[96,128]{1,0:T(8,128)S(1)} %get-tuple-element.17), channel_id=1, source_target_pairs={{0,8},{1,9},{2,10},{3,11},{4,12},{5,13},{6,14},{7,15},{8,16},{9,17... | collective-permute-start | bytes 147464 | tf_op jit(solution)/shard_map/ppermute | solution.py:578
  4.7 6.0 %copy-start.6 = (s32[1536]{0:T(1024)S(1)}, s32[1536]{0:T(1024)}, u32[]{:S(2)}) copy-start(s32[1536]{0:T(1024)} %param.12) | copy-start | bytes 18436
  4.7 8.6 %copy-start.2 = (bf16[64,96,128]{2,1,0:T(8,128)(2,1)S(1)}, bf16[64,96,128]{2,1,0:T(8,128)(2,1)}, u32[]{:S(2)}) copy-start(bf16[64,96,128]{2,1,0:T(8,128)(2,1)} %temper_hbm.1) | copy-start | bytes 4718596
  4.7 8.6 %copy-start.5 = (s32[1536,1]{0,1:T(1,128)S(1)}, s32[1536,1]{0,1:T(1,128)}, u32[]{:S(2)}) copy-start(s32[1536,1]{0,1:T(1,128)} %param.11) | copy-start | bytes 18436
  4.7 6.0 %collective-permute-start.1 = (f32[96,128]{1,0:T(8,128)S(1)}, f32[96,128]{1,0:T(8,128)S(1)}, u32[]{:S(2)}, u32[]{:S(2)}) collective-permute-start(f32[96,128]{1,0:T(8,128)S(1)} %get-tuple-element.18), channel_id=1, source_target_pairs={{0,120},{1,121},{2,122},{3,123},{4,124},{5,125},{6,126},{7,127},{8... | collective-permute-start | bytes 147464 | tf_op jit(solution)/shard_map/ppermute | solution.py:578
  10.7 4.0 %collective-permute-start.2 = (f32[64,128]{1,0:T(8,128)S(1)}, f32[64,128]{1,0:T(8,128)S(1)}, u32[]{:S(2)}, u32[]{:S(2)}) collective-permute-start(f32[64,128]{1,0:T(8,128)S(1)} %get-tuple-element.21), channel_id=1, source_target_pairs={{0,1},{1,2},{2,3},{3,4},{4,5},{5,6},{6,7},{7,0},{8,9},{9,10},{10,1... | collective-permute-start | bytes 98312 | tf_op jit(solution)/shard_map/ppermute | solution.py:578
  13.3 3.3 %collective-permute-start.3 = (f32[64,128]{1,0:T(8,128)S(1)}, f32[64,128]{1,0:T(8,128)S(1)}, u32[]{:S(2)}, u32[]{:S(2)}) collective-permute-start(f32[64,128]{1,0:T(8,128)S(1)} %get-tuple-element.22), channel_id=1, source_target_pairs={{0,7},{1,0},{2,1},{3,2},{4,3},{5,4},{6,5},{7,6},{8,15},{9,8},{10,9... | collective-permute-start | bytes 98312 | tf_op jit(solution)/shard_map/ppermute | solution.py:578
  20.7 36.6 %copy-start.3 = (bf16[256,2048]{1,0:T(8,128)(2,1)S(1)}, bf16[256,2048]{1,0:T(8,128)(2,1)}, u32[]{:S(2)}) copy-start(bf16[256,2048]{1,0:T(8,128)(2,1)} %win_ref.1) | copy-start | bytes 3145732
  20.7 36.5 %copy-start.4 = (bf16[2048,256]{1,0:T(8,128)(2,1)S(1)}, bf16[2048,256]{1,0:T(8,128)(2,1)}, u32[]{:S(2)}) copy-start(bf16[2048,256]{1,0:T(8,128)(2,1)} %wout_ref.1) | copy-start | bytes 3145732

commit v3 on v2

--- a/solution.py
+++ b/solution.py
@@ -47,7 +47,7 @@
 
 def cell_pair(nodes):
     halves = [[combine(PG2[a], [nodes[x][k] for x in range(4)]) for k in range(4)] for a in range(2)]
-    return [[combine(-LOG2E * PG2[b], halves[a]) for b in range(2)] for a in range(2)]
+    return [[combine(PG2[b], halves[a]) for b in range(2)] for a in range(2)]
 
 
 def call(kernel, out_shape, *args, vmem, flops=0, moved=0, **kw):
@@ -410,7 +410,7 @@
 PIECES = 2
 
 
-def radiate_kernel(cap, x_ref, aerosol_hbm, win_ref, wout_ref, out_ref, aerosol_ref,
+def radiate_kernel(cap, x_ref, aerosol_hbm, win_ref, wout_ref, out_ref, aerosol_ref, scaled_ref,
                    depth_a, depth_b, trans_a, trans_b, bound_a, bound_b, sem):
     blocks, rows, width = aerosol_ref.shape
     lev = x_ref.shape[1]
@@ -431,6 +431,13 @@
     for block in range(blocks):
         for copy in fetches(block):
             copy.start()
+
+    deep = win_ref.shape[0]
+    for r in range(0, deep, 32):
+        weight = win_ref[pl.ds(r, 32), :].astype(F32) * -LOG2E
+        high = weight.astype(BF16)
+        scaled_ref[pl.ds(r, 32), :] = high
+        scaled_ref[pl.ds(deep + r, 32), :] = (weight - high.astype(F32)).astype(BF16)
 
     lane = lax.broadcasted_iota(I32, (8, lev), 1)
     sub = lax.broadcasted_iota(I32, (8, lev), 0)
@@ -446,11 +453,12 @@
         state = jnp.concatenate(
             [jnp.concatenate(tracer, axis=0), jnp.concatenate(temper, axis=0)], axis=1
         ).astype(BF16)
+        state = jnp.concatenate([state, state], axis=1)
         mine = jnp.concatenate(mine, axis=0).astype(BF16)
         cost = jnp.dot(mine, ones, preferred_element_type=F32)
         for g in range(1, 4):
             bound[g - 1] = jnp.where(cost > g - 0.5, 120.0, -1e30)
-        depth[...] = jnp.dot(state, win_ref[...], preferred_element_type=F32)
+        depth[...] = jnp.dot(state, scaled_ref[...], preferred_element_type=F32)
 
     def middle(block, depth, bound, trans):
         step, tile = 256, 64
@@ -502,6 +510,7 @@
         in_specs=[in_vmem, pl.BlockSpec(memory_space=pltpu.HBM), in_vmem, in_vmem],
         scratch_shapes=[
             pltpu.VMEM((rows // block, block, width), BF16),
+            pltpu.VMEM((2 * band_in.shape[0], width), BF16),
             pltpu.VMEM((block, width), F32),
             pltpu.VMEM((block, width), F32),
             pltpu.VMEM((block, width), BF16),

time: 103 us -> 105 us (1.019)
  Pallas kernels: 26.2 us -> 28.5 us
    pallas_call x7, Pallas kernels: 26.2 us -> 28.5 us  [call(): pl.pallas_call(kernel, out_shape=out_shape, compiler_params=pltpu.Compile...]
  transfers between devices with their start and end apart: 4 -> 4, of which waited for: 1 -> 1; matrix products, arithmetic and copies ran while one was open for 0% -> 0% of each run, Pallas kernels for 4% -> 3%
where the time goes in v3:
time: 105 us
  blocking collectives  65.4 us (62%)
  Pallas kernels  28.5 us (27%)
  starting transfers between devices  8.46 us (8%)
  waiting for transfers between devices  1.82 us (2%)
    all_to_all x2, blocking collectives, exchange(): lax.all_to_all(x, ('dyn', 'col'), split_axis=0, concat_axis=0, tiled=True)  65.4 us
    pallas_call x7, Pallas kernels, call(): pl.pallas_call(kernel, out_shape=out_shape, compiler_params=pltpu.Compile...  28.5 us
    ppermute x4, starting transfers between devices, send(): return lax.ppermute(x, ('dyn', 'col'), pairs)  8.46 us
  transfers between devices with their start and end apart: 4, of which 1 were waited for; matrix products, arithmetic and copies ran while one was open for 0% of the time, Pallas kernels for 3%

profile of v3, /device:TPU:1, one launch (start us, length us, event | category | flops | bytes accessed | tf_op | source)
XLA Modules:
  0.0 105.2 jit_solution(370608720343797233)
XLA Ops:
  0.6 0.0 copy-start
  0.6 0.0 copy-start.1
  0.6 1.9 %shard_map.96 = (f32[96,128]{1,0:T(8,128)S(1)}, f32[96,128]{1,0:T(8,128)S(1)}, f32[64,128]{1,0:T(8,128)S(1)}, f32[64,128]{1,0:T(8,128)S(1)}) custom-call(bf16[64,96,128]{2,1,0:T(8,128)(2,1)} %tracer.1, bf16[2,64,96,128]{3,2,1,0:T(8,128)(2,1)} %winds.1), custom_call_target="tpu_custom_call" | custom-call | flops 1000000 | bytes 3000000 | tf_op jit(solution)/shard_map/pallas_call | solution.py:54
  2.6 2.1 %collective-permute-start = (f32[96,128]{1,0:T(8,128)S(1)}, f32[96,128]{1,0:T(8,128)S(1)}, u32[]{:S(2)}, u32[]{:S(2)}) collective-permute-start(f32[96,128]{1,0:T(8,128)S(1)} %get-tuple-element.17), channel_id=1, source_target_pairs={{0,8},{1,9},{2,10},{3,11},{4,12},{5,13},{6,14},{7,15},{8,16},{9,17... | collective-permute-start | bytes 147464 | tf_op jit(solution)/shard_map/ppermute | solution.py:587
  4.7 0.0 copy-start.6
  4.7 0.0 copy-start.2
  4.7 0.0 copy-start.5
  4.7 3.8 %collective-permute-start.1 = (f32[96,128]{1,0:T(8,128)S(1)}, f32[96,128]{1,0:T(8,128)S(1)}, u32[]{:S(2)}, u32[]{:S(2)}) collective-permute-start(f32[96,128]{1,0:T(8,128)S(1)} %get-tuple-element.18), channel_id=1, source_target_pairs={{0,120},{1,121},{2,122},{3,123},{4,124},{5,125},{6,126},{7,127},{8... | collective-permute-start | bytes 147464 | tf_op jit(solution)/shard_map/ppermute | solution.py:587
  8.5 0.0 copy-done
  8.5 0.0 copy-done.1
  8.5 2.1 %shard_map.95 = (f32[6144,128]{1,0:T(8,128)S(1)}, f32[6144,128]{1,0:T(8,128)S(1)}) custom-call(bf16[64,96,128]{2,1,0:T(8,128)(2,1)S(1)} %copy-done.1, bf16[2,64,96,128]{3,2,1,0:T(8,128)(2,1)S(1)} %copy-done), custom_call_target="tpu_custom_call" | custom-call | flops 2000000000 | bytes 8000000 | tf_op jit(solution)/shard_map/pallas_call | solution.py:54
  10.7 0.0 copy-done.6
  10.7 0.0 collective-permute-done.xprev
  10.7 0.0 collective-permute-done.1.xnext
  10.7 2.5 %collective-permute-start.2 = (f32[64,128]{1,0:T(8,128)S(1)}, f32[64,128]{1,0:T(8,128)S(1)}, u32[]{:S(2)}, u32[]{:S(2)}) collective-permute-start(f32[64,128]{1,0:T(8,128)S(1)} %get-tuple-element.21), channel_id=1, source_target_pairs={{0,1},{1,2},{2,3},{3,4},{4,5},{5,6},{6,7},{7,0},{8,9},{9,10},{10,1... | collective-permute-start | bytes 98312 | tf_op jit(solution)/shard_map/ppermute | solution.py:587
  13.3 0.0 collective-permute-start.3
  13.3 0.0 copy-done.2
  13.3 0.0 copy-done.5
  13.3 1.5 %shard_map.98 = (s32[1,1536]{1,0:T(1,128)S(1)}, f32[128,128]{1,0:T(8,128)S(1)}, bf16[1536,128]{1,0:T(8,128)(2,1)S(1)}) custom-call(s32[1,1536]{1,0:T(1,128)S(1)} %bitcast.10, s32[1,1536]{1,0:T(1,128)S(1)} %reshape.23.classes_ref, bf16[64,96,128]{2,1,0:T(8,128)(2,1)S(1)} %copy-done.2), custom_call_target="tpu_custom_call" | custom-call | flops 1000000000 | bytes 4000000 | tf_op jit(solution)/shard_map/pallas_call | solution.py:54
  14.8 0.0 collective-permute-done.2.yprev
  14.8 1.8 %collective-permute-done.3.ynext = f32[64,128]{1,0:T(8,128)S(1)} collective-permute-done((f32[64,128]{1,0:T(8,128)S(1)}, f32[64,128]{1,0:T(8,128)S(1)}, u32[]{:S(2)}, u32[]{:S(2)}) %collective-permute-start.3) | collective-permute-done | bytes 32800 | tf_op jit(solution)/shard_map/ppermute | solution.py:587
  16.6 4.1 %shard_map.99 = (bf16[64,96,128]{2,1,0:T(8,128)(2,1)}, bf16[7168,128]{1,0:T(8,128)(2,1)S(1)}) custom-call(f32[6144,128]{1,0:T(8,128)S(1)} %get-tuple-element.15.nodes_ref, f32[6144,128]{1,0:T(8,128)S(1)} %get-tuple-element.16.tend_ref, f32[96,128]{1,0:T(8,128)S(1)} %collective-permute-done.xprev, f32[96,128]{1,0:T(8,128)S(1)} %collective-permute-done.1.xnext, ...), custom_call_target="tpu_custom_call" | custom-call | flops 4000000000 | bytes 8000000 | tf_op jit(solution)/shard_map/pallas_call | solution.py:54
  20.7 0.0 copy-start.3
  20.7 0.0 copy-start.4
  20.7 36.5 %all_to_all.10 = bf16[128,56,128]{2,1,0:T(8,128)(2,1)S(1)} all-to-all(bf16[128,56,128]{2,1,0:T(8,128)(2,1)S(1)} %bitcast.6), channel_id=1, replica_groups=mesh['dyn'=16,'col'=8] {'dyn','col'}, dimensions={0} | all-to-all | bytes 3670016 | tf_op jit(solution)/shard_map/all_to_all | solution.py:572
  57.2 0.0 copy-done.3
  57.2 0.0 copy-done.4
  57.2 15.2 %shard_map.100 = bf16[3072,256]{1,0:T(8,128)(2,1)S(1)} custom-call(bf16[7168,128]{1,0:T(8,128)(2,1)S(1)} %bitcast.7, bf16[3072,2048]{1,0:T(8,128)(2,1)} %bitcast.13, bf16[256,2048]{1,0:T(8,128)(2,1)S(1)} %copy-done.3, bf16[2048,256]{1,0:T(8,128)(2,1)S(1)} %copy-done.4), custom_call_target="tpu_custom_call" | custom-call | flops 7000000000 | bytes 20000000 | tf_op jit(solution)/shard_map/pallas_call | solution.py:54
  72.4 28.9 %all_to_all.11 = bf16[128,24,256]{2,1,0:T(8,128)(2,1)S(1)} all-to-all(bf16[128,24,256]{2,1,0:T(8,128)(2,1)S(1)} %bitcast.9), channel_id=1, replica_groups=mesh['dyn'=16,'col'=8] {'dyn','col'}, dimensions={0} | all-to-all | bytes 3145728 | tf_op jit(solution)/shard_map/all_to_all | solution.py:572
  101.3 3.7 %shard_map.101 = bf16[1536,256]{1,0:T(8,128)(2,1)} custom-call(s32[1,1536]{1,0:T(1,128)S(1)} %bitcast.12, s32[1,1536]{1,0:T(1,128)S(1)} %get-tuple-element.23.slot_ref, bf16[3072,256]{1,0:T(8,128)(2,1)S(1)} %bitcast.8), custom_call_target="tpu_custom_call" | custom-call | flops 3000000000 | bytes 3000000 | tf_op jit(solution)/shard_map/pallas_call | solution.py:54
  (2 shorter events, 0.0 us)
Async XLA Ops:
  0.6 7.9 %copy-start = (bf16[2,64,96,128]{3,2,1,0:T(8,128)(2,1)S(1)}, bf16[2,64,96,128]{3,2,1,0:T(8,128)(2,1)}, u32[]{:S(2)}) copy-start(bf16[2,64,96,128]{3,2,1,0:T(8,128)(2,1)} %winds.1) | copy-start | bytes 9437188
  0.6 7.9 %copy-start.1 = (bf16[64,96,128]{2,1,0:T(8,128)(2,1)S(1)}, bf16[64,96,128]{2,1,0:T(8,128)(2,1)}, u32[]{:S(2)}) copy-start(bf16[64,96,128]{2,1,0:T(8,128)(2,1)} %tracer.1) | copy-start | bytes 4718596
  2.6 8.1 %collective-permute-start = (f32[96,128]{1,0:T(8,128)S(1)}, f32[96,128]{1,0:T(8,128)S(1)}, u32[]{:S(2)}, u32[]{:S(2)}) collective-permute-start(f32[96,128]{1,0:T(8,128)S(1)} %get-tuple-element.17), channel_id=1, source_target_pairs={{0,8},{1,9},{2,10},{3,11},{4,12},{5,13},{6,14},{7,15},{8,16},{9,17... | collective-permute-start | bytes 147464 | tf_op jit(solution)/shard_map/ppermute | solution.py:587
  4.7 6.0 %copy-start.6 = (s32[1536]{0:T(1024)S(1)}, s32[1536]{0:T(1024)}, u32[]{:S(2)}) copy-start(s32[1536]{0:T(1024)} %param.12) | copy-start | bytes 18436
  4.7 8.6 %copy-start.2 = (bf16[64,96,128]{2,1,0:T(8,128)(2,1)S(1)}, bf16[64,96,128]{2,1,0:T(8,128)(2,1)}, u32[]{:S(2)}) copy-start(bf16[64,96,128]{2,1,0:T(8,128)(2,1)} %temper_hbm.1) | copy-start | bytes 4718596
  4.7 8.6 %copy-start.5 = (s32[1536,1]{0,1:T(1,128)S(1)}, s32[1536,1]{0,1:T(1,128)}, u32[]{:S(2)}) copy-start(s32[1536,1]{0,1:T(1,128)} %param.11) | copy-start | bytes 18436
  4.7 6.0 %collective-permute-start.1 = (f32[96,128]{1,0:T(8,128)S(1)}, f32[96,128]{1,0:T(8,128)S(1)}, u32[]{:S(2)}, u32[]{:S(2)}) collective-permute-start(f32[96,128]{1,0:T(8,128)S(1)} %get-tuple-element.18), channel_id=1, source_target_pairs={{0,120},{1,121},{2,122},{3,123},{4,124},{5,125},{6,126},{7,127},{8... | collective-permute-start | bytes 147464 | tf_op jit(solution)/shard_map/ppermute | solution.py:587
  10.7 4.0 %collective-permute-start.2 = (f32[64,128]{1,0:T(8,128)S(1)}, f32[64,128]{1,0:T(8,128)S(1)}, u32[]{:S(2)}, u32[]{:S(2)}) collective-permute-start(f32[64,128]{1,0:T(8,128)S(1)} %get-tuple-element.21), channel_id=1, source_target_pairs={{0,1},{1,2},{2,3},{3,4},{4,5},{5,6},{6,7},{7,0},{8,9},{9,10},{10,1... | collective-permute-start | bytes 98312 | tf_op jit(solution)/shard_map/ppermute | solution.py:587
  13.3 3.3 %collective-permute-start.3 = (f32[64,128]{1,0:T(8,128)S(1)}, f32[64,128]{1,0:T(8,128)S(1)}, u32[]{:S(2)}, u32[]{:S(2)}) collective-permute-start(f32[64,128]{1,0:T(8,128)S(1)} %get-tuple-element.22), channel_id=1, source_target_pairs={{0,7},{1,0},{2,1},{3,2},{4,3},{5,4},{6,5},{7,6},{8,15},{9,8},{10,9... | collective-permute-start | bytes 98312 | tf_op jit(solution)/shard_map/ppermute | solution.py:587
  20.7 36.6 %copy-start.3 = (bf16[256,2048]{1,0:T(8,128)(2,1)S(1)}, bf16[256,2048]{1,0:T(8,128)(2,1)}, u32[]{:S(2)}) copy-start(bf16[256,2048]{1,0:T(8,128)(2,1)} %win_ref.1) | copy-start | bytes 3145732
  20.7 36.5 %copy-start.4 = (bf16[2048,256]{1,0:T(8,128)(2,1)S(1)}, bf16[2048,256]{1,0:T(8,128)(2,1)}, u32[]{:S(2)}) copy-start(bf16[2048,256]{1,0:T(8,128)(2,1)} %wout_ref.1) | copy-start | bytes 3145732

commit v4 on v2

--- a/solution.py
+++ b/solution.py
@@ -47,7 +47,7 @@
 
 def cell_pair(nodes):
     halves = [[combine(PG2[a], [nodes[x][k] for x in range(4)]) for k in range(4)] for a in range(2)]
-    return [[combine(-LOG2E * PG2[b], halves[a]) for b in range(2)] for a in range(2)]
+    return [[combine(PG2[b], halves[a]) for b in range(2)] for a in range(2)]
 
 
 def call(kernel, out_shape, *args, vmem, flops=0, moved=0, **kw):
@@ -436,30 +436,37 @@
     sub = lax.broadcasted_iota(I32, (8, lev), 0)
     ones = jnp.ones((lev, lev), BF16)
 
-    def begin(block, depth, bound):
+    def begin(block, bound):
         tracer, temper, mine = [], [], []
         for s in range(sources):
             lines = x_ref[pl.ds((block * sources + s) * each, each), :].astype(F32)
             tracer.append(lines[:cap])
             temper.append(lines[cap : 2 * cap])
             mine += [jnp.where(lane == sub + 8 * j, lines[2 * cap :], 0.0) for j in range(cap // 8)]
-        state = jnp.concatenate(
+        state = -jnp.concatenate(
             [jnp.concatenate(tracer, axis=0), jnp.concatenate(temper, axis=0)], axis=1
         ).astype(BF16)
         mine = jnp.concatenate(mine, axis=0).astype(BF16)
         cost = jnp.dot(mine, ones, preferred_element_type=F32)
         for g in range(1, 4):
             bound[g - 1] = jnp.where(cost > g - 0.5, 120.0, -1e30)
-        depth[...] = jnp.dot(state, win_ref[...], preferred_element_type=F32)
-
-    def middle(block, depth, bound, trans):
-        step, tile = 256, 64
-        parts = width // step
-        for i, r in [(i, r) for i in range(parts) for r in range(0, rows, tile)]:
+        return state
+
+    half = width // 2
+
+    def deepen(state, depth, h):
+        at = pl.ds(h * half, half)
+        depth[:, at] = jnp.dot(state, win_ref[:, at], preferred_element_type=F32)
+
+    step, tile = 256, 64
+    parts = width // step
+
+    def middle(block, depth, bound, trans, chunks):
+        for i, r in [(i, r) for i in chunks for r in range(0, rows, tile)]:
             at, line = pl.ds(i * step, step), pl.ds(r, tile)
             group = i * 4 // parts
             top = jnp.concatenate([bound[group - 1, line]] * (step // lev), axis=1) if group else 120.0
-            capped = jnp.minimum(depth[line, at], top)
+            capped = jnp.minimum(depth[line, at] * LOG2E, top)
             soft = capped - jnp.log2(1.0 + jnp.exp2(capped))
             kept = jnp.exp2(soft * aerosol_ref[block, line, at].astype(F32)).astype(BF16)
             trans[line, at] = kept
@@ -469,20 +476,27 @@
             trans[...], wout_ref[...], preferred_element_type=F32
         ).astype(BF16)
 
-    begin(0, depth_a, bound_a)
+    def advance(block, following, depth, bound, trans, depth_next, bound_next, before, trans_before):
+        for copy in fetches(block):
+            copy.wait()
+        state = begin(following, bound_next)
+        deepen(state, depth_next, 0)
+        middle(block, depth, bound, trans, range(0, 3))
+        finish(before, trans_before)
+        middle(block, depth, bound, trans, range(3, 6))
+        deepen(state, depth_next, 1)
+        middle(block, depth, bound, trans, range(6, parts))
+
+    state = begin(0, bound_a)
+    deepen(state, depth_a, 0)
+    deepen(state, depth_a, 1)
 
     def pair(i, _):
         first = 2 * i
-        for copy in fetches(first):
-            copy.wait()
-        begin(first + 1, depth_b, bound_b)
-        finish(jnp.maximum(first - 1, 0), trans_b)
-        middle(first, depth_a, bound_a, trans_a)
-        for copy in fetches(first + 1):
-            copy.wait()
-        begin(jnp.minimum(first + 2, blocks - 1), depth_a, bound_a)
-        finish(first, trans_a)
-        middle(first + 1, depth_b, bound_b, trans_b)
+        later = jnp.minimum(first + 2, blocks - 1)
+        before = jnp.maximum(first - 1, 0)
+        advance(first, first + 1, depth_a, bound_a, trans_a, depth_b, bound_b, before, trans_b)
+        advance(first + 1, later, depth_b, bound_b, trans_b, depth_a, bound_a, first, trans_a)
         return 0
 
     lax.fori_loop(0, blocks // 2, pair, 0)

time: 103 us -> 103 us (level)
  no operation moved by 1% of the time
where the time goes in v4:
time: 103 us
  blocking collectives  65.4 us (63%)
  Pallas kernels  26.5 us (26%)
  starting transfers between devices  8.46 us (8%)
  waiting for transfers between devices  1.82 us (2%)
    all_to_all x2, blocking collectives, exchange(): lax.all_to_all(x, ('dyn', 'col'), split_axis=0, concat_axis=0, tiled=True)  65.4 us
    pallas_call x7, Pallas kernels, call(): pl.pallas_call(kernel, out_shape=out_shape, compiler_params=pltpu.Compile...  26.5 us
    ppermute x4, starting transfers between devices, send(): return lax.ppermute(x, ('dyn', 'col'), pairs)  8.46 us
  transfers between devices with their start and end apart: 4, of which 1 were waited for; matrix products, arithmetic and copies ran while one was open for 0% of the time, Pallas kernels for 4%

profile of v4, /device:TPU:1, one launch (start us, length us, event | category | flops | bytes accessed | tf_op | source)
XLA Modules:
  0.0 103.1 jit_solution(18218800337510990382)
XLA Ops:
  0.6 0.0 copy-start
  0.6 0.0 copy-start.1
  0.6 1.9 %shard_map.96 = (f32[96,128]{1,0:T(8,128)S(1)}, f32[96,128]{1,0:T(8,128)S(1)}, f32[64,128]{1,0:T(8,128)S(1)}, f32[64,128]{1,0:T(8,128)S(1)}) custom-call(bf16[64,96,128]{2,1,0:T(8,128)(2,1)} %tracer.1, bf16[2,64,96,128]{3,2,1,0:T(8,128)(2,1)} %winds.1), custom_call_target="tpu_custom_call" | custom-call | flops 1000000 | bytes 3000000 | tf_op jit(solution)/shard_map/pallas_call | solution.py:54
  2.6 2.1 %collective-permute-start = (f32[96,128]{1,0:T(8,128)S(1)}, f32[96,128]{1,0:T(8,128)S(1)}, u32[]{:S(2)}, u32[]{:S(2)}) collective-permute-start(f32[96,128]{1,0:T(8,128)S(1)} %get-tuple-element.17), channel_id=1, source_target_pairs={{0,8},{1,9},{2,10},{3,11},{4,12},{5,13},{6,14},{7,15},{8,16},{9,17... | collective-permute-start | bytes 147464 | tf_op jit(solution)/shard_map/ppermute | solution.py:592
  4.7 0.0 copy-start.6
  4.7 0.0 copy-start.2
  4.7 0.0 copy-start.5
  4.7 3.8 %collective-permute-start.1 = (f32[96,128]{1,0:T(8,128)S(1)}, f32[96,128]{1,0:T(8,128)S(1)}, u32[]{:S(2)}, u32[]{:S(2)}) collective-permute-start(f32[96,128]{1,0:T(8,128)S(1)} %get-tuple-element.18), channel_id=1, source_target_pairs={{0,120},{1,121},{2,122},{3,123},{4,124},{5,125},{6,126},{7,127},{8... | collective-permute-start | bytes 147464 | tf_op jit(solution)/shard_map/ppermute | solution.py:592
  8.5 0.0 copy-done
  8.5 0.0 copy-done.1
  8.5 2.1 %shard_map.95 = (f32[6144,128]{1,0:T(8,128)S(1)}, f32[6144,128]{1,0:T(8,128)S(1)}) custom-call(bf16[64,96,128]{2,1,0:T(8,128)(2,1)S(1)} %copy-done.1, bf16[2,64,96,128]{3,2,1,0:T(8,128)(2,1)S(1)} %copy-done), custom_call_target="tpu_custom_call" | custom-call | flops 2000000000 | bytes 8000000 | tf_op jit(solution)/shard_map/pallas_call | solution.py:54
  10.7 0.0 copy-done.6
  10.7 0.0 collective-permute-done.xprev
  10.7 0.0 collective-permute-done.1.xnext
  10.7 2.5 %collective-permute-start.2 = (f32[64,128]{1,0:T(8,128)S(1)}, f32[64,128]{1,0:T(8,128)S(1)}, u32[]{:S(2)}, u32[]{:S(2)}) collective-permute-start(f32[64,128]{1,0:T(8,128)S(1)} %get-tuple-element.21), channel_id=1, source_target_pairs={{0,1},{1,2},{2,3},{3,4},{4,5},{5,6},{6,7},{7,0},{8,9},{9,10},{10,1... | collective-permute-start | bytes 98312 | tf_op jit(solution)/shard_map/ppermute | solution.py:592
  13.3 0.0 collective-permute-start.3
  13.3 0.0 copy-done.2
  13.3 0.0 copy-done.5
  13.3 1.5 %shard_map.98 = (s32[1,1536]{1,0:T(1,128)S(1)}, f32[128,128]{1,0:T(8,128)S(1)}, bf16[1536,128]{1,0:T(8,128)(2,1)S(1)}) custom-call(s32[1,1536]{1,0:T(1,128)S(1)} %bitcast.10, s32[1,1536]{1,0:T(1,128)S(1)} %reshape.23.classes_ref, bf16[64,96,128]{2,1,0:T(8,128)(2,1)S(1)} %copy-done.2), custom_call_target="tpu_custom_call" | custom-call | flops 1000000000 | bytes 4000000 | tf_op jit(solution)/shard_map/pallas_call | solution.py:54
  14.8 0.0 collective-permute-done.2.yprev
  14.8 1.8 %collective-permute-done.3.ynext = f32[64,128]{1,0:T(8,128)S(1)} collective-permute-done((f32[64,128]{1,0:T(8,128)S(1)}, f32[64,128]{1,0:T(8,128)S(1)}, u32[]{:S(2)}, u32[]{:S(2)}) %collective-permute-start.3) | collective-permute-done | bytes 32800 | tf_op jit(solution)/shard_map/ppermute | solution.py:592
  16.6 4.1 %shard_map.99 = (bf16[64,96,128]{2,1,0:T(8,128)(2,1)}, bf16[7168,128]{1,0:T(8,128)(2,1)S(1)}) custom-call(f32[6144,128]{1,0:T(8,128)S(1)} %get-tuple-element.15.nodes_ref, f32[6144,128]{1,0:T(8,128)S(1)} %get-tuple-element.16.tend_ref, f32[96,128]{1,0:T(8,128)S(1)} %collective-permute-done.xprev, f32[96,128]{1,0:T(8,128)S(1)} %collective-permute-done.1.xnext, ...), custom_call_target="tpu_custom_call" | custom-call | flops 4000000000 | bytes 8000000 | tf_op jit(solution)/shard_map/pallas_call | solution.py:54
  20.7 0.0 copy-start.3
  20.7 0.0 copy-start.4
  20.7 36.5 %all_to_all.10 = bf16[128,56,128]{2,1,0:T(8,128)(2,1)S(1)} all-to-all(bf16[128,56,128]{2,1,0:T(8,128)(2,1)S(1)} %bitcast.6), channel_id=1, replica_groups=mesh['dyn'=16,'col'=8] {'dyn','col'}, dimensions={0} | all-to-all | bytes 3670016 | tf_op jit(solution)/shard_map/all_to_all | solution.py:577
  57.2 0.0 copy-done.3
  57.2 0.0 copy-done.4
  57.2 13.1 %shard_map.100 = bf16[3072,256]{1,0:T(8,128)(2,1)S(1)} custom-call(bf16[7168,128]{1,0:T(8,128)(2,1)S(1)} %bitcast.7, bf16[3072,2048]{1,0:T(8,128)(2,1)} %bitcast.13, bf16[256,2048]{1,0:T(8,128)(2,1)S(1)} %copy-done.3, bf16[2048,256]{1,0:T(8,128)(2,1)S(1)} %copy-done.4), custom_call_target="tpu_custom_call" | custom-call | flops 7000000000 | bytes 20000000 | tf_op jit(solution)/shard_map/pallas_call | solution.py:54
  70.3 28.9 %all_to_all.11 = bf16[128,24,256]{2,1,0:T(8,128)(2,1)S(1)} all-to-all(bf16[128,24,256]{2,1,0:T(8,128)(2,1)S(1)} %bitcast.9), channel_id=1, replica_groups=mesh['dyn'=16,'col'=8] {'dyn','col'}, dimensions={0} | all-to-all | bytes 3145728 | tf_op jit(solution)/shard_map/all_to_all | solution.py:577
  99.2 3.7 %shard_map.101 = bf16[1536,256]{1,0:T(8,128)(2,1)} custom-call(s32[1,1536]{1,0:T(1,128)S(1)} %bitcast.12, s32[1,1536]{1,0:T(1,128)S(1)} %get-tuple-element.23.slot_ref, bf16[3072,256]{1,0:T(8,128)(2,1)S(1)} %bitcast.8), custom_call_target="tpu_custom_call" | custom-call | flops 3000000000 | bytes 3000000 | tf_op jit(solution)/shard_map/pallas_call | solution.py:54
  (2 shorter events, 0.0 us)
Async XLA Ops:
  0.6 7.9 %copy-start = (bf16[2,64,96,128]{3,2,1,0:T(8,128)(2,1)S(1)}, bf16[2,64,96,128]{3,2,1,0:T(8,128)(2,1)}, u32[]{:S(2)}) copy-start(bf16[2,64,96,128]{3,2,1,0:T(8,128)(2,1)} %winds.1) | copy-start | bytes 9437188
  0.6 7.9 %copy-start.1 = (bf16[64,96,128]{2,1,0:T(8,128)(2,1)S(1)}, bf16[64,96,128]{2,1,0:T(8,128)(2,1)}, u32[]{:S(2)}) copy-start(bf16[64,96,128]{2,1,0:T(8,128)(2,1)} %tracer.1) | copy-start | bytes 4718596
  2.6 8.1 %collective-permute-start = (f32[96,128]{1,0:T(8,128)S(1)}, f32[96,128]{1,0:T(8,128)S(1)}, u32[]{:S(2)}, u32[]{:S(2)}) collective-permute-start(f32[96,128]{1,0:T(8,128)S(1)} %get-tuple-element.17), channel_id=1, source_target_pairs={{0,8},{1,9},{2,10},{3,11},{4,12},{5,13},{6,14},{7,15},{8,16},{9,17... | collective-permute-start | bytes 147464 | tf_op jit(solution)/shard_map/ppermute | solution.py:592
  4.7 6.0 %copy-start.6 = (s32[1536]{0:T(1024)S(1)}, s32[1536]{0:T(1024)}, u32[]{:S(2)}) copy-start(s32[1536]{0:T(1024)} %param.12) | copy-start | bytes 18436
  4.7 8.6 %copy-start.2 = (bf16[64,96,128]{2,1,0:T(8,128)(2,1)S(1)}, bf16[64,96,128]{2,1,0:T(8,128)(2,1)}, u32[]{:S(2)}) copy-start(bf16[64,96,128]{2,1,0:T(8,128)(2,1)} %temper_hbm.1) | copy-start | bytes 4718596
  4.7 8.6 %copy-start.5 = (s32[1536,1]{0,1:T(1,128)S(1)}, s32[1536,1]{0,1:T(1,128)}, u32[]{:S(2)}) copy-start(s32[1536,1]{0,1:T(1,128)} %param.11) | copy-start | bytes 18436
  4.7 6.0 %collective-permute-start.1 = (f32[96,128]{1,0:T(8,128)S(1)}, f32[96,128]{1,0:T(8,128)S(1)}, u32[]{:S(2)}, u32[]{:S(2)}) collective-permute-start(f32[96,128]{1,0:T(8,128)S(1)} %get-tuple-element.18), channel_id=1, source_target_pairs={{0,120},{1,121},{2,122},{3,123},{4,124},{5,125},{6,126},{7,127},{8... | collective-permute-start | bytes 147464 | tf_op jit(solution)/shard_map/ppermute | solution.py:592
  10.7 4.0 %collective-permute-start.2 = (f32[64,128]{1,0:T(8,128)S(1)}, f32[64,128]{1,0:T(8,128)S(1)}, u32[]{:S(2)}, u32[]{:S(2)}) collective-permute-start(f32[64,128]{1,0:T(8,128)S(1)} %get-tuple-element.21), channel_id=1, source_target_pairs={{0,1},{1,2},{2,3},{3,4},{4,5},{5,6},{6,7},{7,0},{8,9},{9,10},{10,1... | collective-permute-start | bytes 98312 | tf_op jit(solution)/shard_map/ppermute | solution.py:592
  13.3 3.3 %collective-permute-start.3 = (f32[64,128]{1,0:T(8,128)S(1)}, f32[64,128]{1,0:T(8,128)S(1)}, u32[]{:S(2)}, u32[]{:S(2)}) collective-permute-start(f32[64,128]{1,0:T(8,128)S(1)} %get-tuple-element.22), channel_id=1, source_target_pairs={{0,7},{1,0},{2,1},{3,2},{4,3},{5,4},{6,5},{7,6},{8,15},{9,8},{10,9... | collective-permute-start | bytes 98312 | tf_op jit(solution)/shard_map/ppermute | solution.py:592
  20.7 36.6 %copy-start.3 = (bf16[256,2048]{1,0:T(8,128)(2,1)S(1)}, bf16[256,2048]{1,0:T(8,128)(2,1)}, u32[]{:S(2)}) copy-start(bf16[256,2048]{1,0:T(8,128)(2,1)} %win_ref.1) | copy-start | bytes 3145732
  20.7 36.5 %copy-start.4 = (bf16[2048,256]{1,0:T(8,128)(2,1)S(1)}, bf16[2048,256]{1,0:T(8,128)(2,1)}, u32[]{:S(2)}) copy-start(bf16[2048,256]{1,0:T(8,128)(2,1)} %wout_ref.1) | copy-start | bytes 3145732

commit v5 on v4

--- a/solution.py
+++ b/solution.py
@@ -471,9 +471,11 @@
             kept = jnp.exp2(soft * aerosol_ref[block, line, at].astype(F32)).astype(BF16)
             trans[line, at] = kept
 
-    def finish(block, trans):
-        out_ref[pl.ds(block * rows, rows), :] = jnp.dot(
-            trans[...], wout_ref[...], preferred_element_type=F32
+    size = rows // 2
+
+    def finish(block, trans, h):
+        out_ref[pl.ds(block * rows + h * size, size), :] = jnp.dot(
+            trans[pl.ds(h * size, size), :], wout_ref[...], preferred_element_type=F32
         ).astype(BF16)
 
     def advance(block, following, depth, bound, trans, depth_next, bound_next, before, trans_before):
@@ -481,9 +483,11 @@
             copy.wait()
         state = begin(following, bound_next)
         deepen(state, depth_next, 0)
-        middle(block, depth, bound, trans, range(0, 3))
-        finish(before, trans_before)
-        middle(block, depth, bound, trans, range(3, 6))
+        middle(block, depth, bound, trans, range(0, 2))
+        finish(before, trans_before, 0)
+        middle(block, depth, bound, trans, range(2, 4))
+        finish(before, trans_before, 1)
+        middle(block, depth, bound, trans, range(4, 6))
         deepen(state, depth_next, 1)
         middle(block, depth, bound, trans, range(6, parts))
 
@@ -500,7 +504,8 @@
         return 0
 
     lax.fori_loop(0, blocks // 2, pair, 0)
-    finish(blocks - 1, trans_b)
+    finish(blocks - 1, trans_b, 0)
+    finish(blocks - 1, trans_b, 1)
 
 
 def radiate(arrived, aerosol, band_in, band_out, cap):

time: 103 us -> 103 us (level)
  no operation moved by 1% of the time
where the time goes in v5:
time: 103 us
  blocking collectives  65.4 us (63%)
  Pallas kernels  26.4 us (26%)
  starting transfers between devices  8.46 us (8%)
  waiting for transfers between devices  1.82 us (2%)
    all_to_all x2, blocking collectives, exchange(): lax.all_to_all(x, ('dyn', 'col'), split_axis=0, concat_axis=0, tiled=True)  65.4 us
    pallas_call x7, Pallas kernels, call(): pl.pallas_call(kernel, out_shape=out_shape, compiler_params=pltpu.Compile...  26.4 us
    ppermute x4, starting transfers between devices, send(): return lax.ppermute(x, ('dyn', 'col'), pairs)  8.46 us
  transfers between devices with their start and end apart: 4, of which 1 were waited for; matrix products, arithmetic and copies ran while one was open for 0% of the time, Pallas kernels for 4%

profile of v5, /device:TPU:1, one launch (start us, length us, event | category | flops | bytes accessed | tf_op | source)
XLA Modules:
  0.0 103.0 jit_solution(3439483394920834154)
XLA Ops:
  0.6 0.0 copy-start
  0.6 0.0 copy-start.1
  0.6 1.9 %shard_map.96 = (f32[96,128]{1,0:T(8,128)S(1)}, f32[96,128]{1,0:T(8,128)S(1)}, f32[64,128]{1,0:T(8,128)S(1)}, f32[64,128]{1,0:T(8,128)S(1)}) custom-call(bf16[64,96,128]{2,1,0:T(8,128)(2,1)} %tracer.1, bf16[2,64,96,128]{3,2,1,0:T(8,128)(2,1)} %winds.1), custom_call_target="tpu_custom_call" | custom-call | flops 1000000 | bytes 3000000 | tf_op jit(solution)/shard_map/pallas_call | solution.py:54
  2.6 2.1 %collective-permute-start = (f32[96,128]{1,0:T(8,128)S(1)}, f32[96,128]{1,0:T(8,128)S(1)}, u32[]{:S(2)}, u32[]{:S(2)}) collective-permute-start(f32[96,128]{1,0:T(8,128)S(1)} %get-tuple-element.17), channel_id=1, source_target_pairs={{0,8},{1,9},{2,10},{3,11},{4,12},{5,13},{6,14},{7,15},{8,16},{9,17... | collective-permute-start | bytes 147464 | tf_op jit(solution)/shard_map/ppermute | solution.py:597
  4.7 0.0 copy-start.6
  4.7 0.0 copy-start.2
  4.7 0.0 copy-start.5
  4.7 3.8 %collective-permute-start.1 = (f32[96,128]{1,0:T(8,128)S(1)}, f32[96,128]{1,0:T(8,128)S(1)}, u32[]{:S(2)}, u32[]{:S(2)}) collective-permute-start(f32[96,128]{1,0:T(8,128)S(1)} %get-tuple-element.18), channel_id=1, source_target_pairs={{0,120},{1,121},{2,122},{3,123},{4,124},{5,125},{6,126},{7,127},{8... | collective-permute-start | bytes 147464 | tf_op jit(solution)/shard_map/ppermute | solution.py:597
  8.5 0.0 copy-done
  8.5 0.0 copy-done.1
  8.5 2.1 %shard_map.95 = (f32[6144,128]{1,0:T(8,128)S(1)}, f32[6144,128]{1,0:T(8,128)S(1)}) custom-call(bf16[64,96,128]{2,1,0:T(8,128)(2,1)S(1)} %copy-done.1, bf16[2,64,96,128]{3,2,1,0:T(8,128)(2,1)S(1)} %copy-done), custom_call_target="tpu_custom_call" | custom-call | flops 2000000000 | bytes 8000000 | tf_op jit(solution)/shard_map/pallas_call | solution.py:54
  10.7 0.0 copy-done.6
  10.7 0.0 collective-permute-done.xprev
  10.7 0.0 collective-permute-done.1.xnext
  10.7 2.5 %collective-permute-start.2 = (f32[64,128]{1,0:T(8,128)S(1)}, f32[64,128]{1,0:T(8,128)S(1)}, u32[]{:S(2)}, u32[]{:S(2)}) collective-permute-start(f32[64,128]{1,0:T(8,128)S(1)} %get-tuple-element.21), channel_id=1, source_target_pairs={{0,1},{1,2},{2,3},{3,4},{4,5},{5,6},{6,7},{7,0},{8,9},{9,10},{10,1... | collective-permute-start | bytes 98312 | tf_op jit(solution)/shard_map/ppermute | solution.py:597
  13.3 0.0 collective-permute-start.3
  13.3 0.0 copy-done.2
  13.3 0.0 copy-done.5
  13.3 1.5 %shard_map.98 = (s32[1,1536]{1,0:T(1,128)S(1)}, f32[128,128]{1,0:T(8,128)S(1)}, bf16[1536,128]{1,0:T(8,128)(2,1)S(1)}) custom-call(s32[1,1536]{1,0:T(1,128)S(1)} %bitcast.10, s32[1,1536]{1,0:T(1,128)S(1)} %reshape.23.classes_ref, bf16[64,96,128]{2,1,0:T(8,128)(2,1)S(1)} %copy-done.2), custom_call_target="tpu_custom_call" | custom-call | flops 1000000000 | bytes 4000000 | tf_op jit(solution)/shard_map/pallas_call | solution.py:54
  14.8 0.0 collective-permute-done.2.yprev
  14.8 1.8 %collective-permute-done.3.ynext = f32[64,128]{1,0:T(8,128)S(1)} collective-permute-done((f32[64,128]{1,0:T(8,128)S(1)}, f32[64,128]{1,0:T(8,128)S(1)}, u32[]{:S(2)}, u32[]{:S(2)}) %collective-permute-start.3) | collective-permute-done | bytes 32800 | tf_op jit(solution)/shard_map/ppermute | solution.py:597
  16.6 4.1 %shard_map.99 = (bf16[64,96,128]{2,1,0:T(8,128)(2,1)}, bf16[7168,128]{1,0:T(8,128)(2,1)S(1)}) custom-call(f32[6144,128]{1,0:T(8,128)S(1)} %get-tuple-element.15.nodes_ref, f32[6144,128]{1,0:T(8,128)S(1)} %get-tuple-element.16.tend_ref, f32[96,128]{1,0:T(8,128)S(1)} %collective-permute-done.xprev, f32[96,128]{1,0:T(8,128)S(1)} %collective-permute-done.1.xnext, ...), custom_call_target="tpu_custom_call" | custom-call | flops 4000000000 | bytes 8000000 | tf_op jit(solution)/shard_map/pallas_call | solution.py:54
  20.7 0.0 copy-start.3
  20.7 0.0 copy-start.4
  20.7 36.5 %all_to_all.10 = bf16[128,56,128]{2,1,0:T(8,128)(2,1)S(1)} all-to-all(bf16[128,56,128]{2,1,0:T(8,128)(2,1)S(1)} %bitcast.6), channel_id=1, replica_groups=mesh['dyn'=16,'col'=8] {'dyn','col'}, dimensions={0} | all-to-all | bytes 3670016 | tf_op jit(solution)/shard_map/all_to_all | solution.py:582
  57.2 0.0 copy-done.3
  57.2 0.0 copy-done.4
  57.2 13.0 %shard_map.100 = bf16[3072,256]{1,0:T(8,128)(2,1)S(1)} custom-call(bf16[7168,128]{1,0:T(8,128)(2,1)S(1)} %bitcast.7, bf16[3072,2048]{1,0:T(8,128)(2,1)} %bitcast.13, bf16[256,2048]{1,0:T(8,128)(2,1)S(1)} %copy-done.3, bf16[2048,256]{1,0:T(8,128)(2,1)S(1)} %copy-done.4), custom_call_target="tpu_custom_call" | custom-call | flops 7000000000 | bytes 20000000 | tf_op jit(solution)/shard_map/pallas_call | solution.py:54
  70.3 28.8 %all_to_all.11 = bf16[128,24,256]{2,1,0:T(8,128)(2,1)S(1)} all-to-all(bf16[128,24,256]{2,1,0:T(8,128)(2,1)S(1)} %bitcast.9), channel_id=1, replica_groups=mesh['dyn'=16,'col'=8] {'dyn','col'}, dimensions={0} | all-to-all | bytes 3145728 | tf_op jit(solution)/shard_map/all_to_all | solution.py:582
  99.1 3.7 %shard_map.101 = bf16[1536,256]{1,0:T(8,128)(2,1)} custom-call(s32[1,1536]{1,0:T(1,128)S(1)} %bitcast.12, s32[1,1536]{1,0:T(1,128)S(1)} %get-tuple-element.23.slot_ref, bf16[3072,256]{1,0:T(8,128)(2,1)S(1)} %bitcast.8), custom_call_target="tpu_custom_call" | custom-call | flops 3000000000 | bytes 3000000 | tf_op jit(solution)/shard_map/pallas_call | solution.py:54
  (2 shorter events, 0.0 us)
Async XLA Ops:
  0.6 7.9 %copy-start = (bf16[2,64,96,128]{3,2,1,0:T(8,128)(2,1)S(1)}, bf16[2,64,96,128]{3,2,1,0:T(8,128)(2,1)}, u32[]{:S(2)}) copy-start(bf16[2,64,96,128]{3,2,1,0:T(8,128)(2,1)} %winds.1) | copy-start | bytes 9437188
  0.6 7.9 %copy-start.1 = (bf16[64,96,128]{2,1,0:T(8,128)(2,1)S(1)}, bf16[64,96,128]{2,1,0:T(8,128)(2,1)}, u32[]{:S(2)}) copy-start(bf16[64,96,128]{2,1,0:T(8,128)(2,1)} %tracer.1) | copy-start | bytes 4718596
  2.6 8.1 %collective-permute-start = (f32[96,128]{1,0:T(8,128)S(1)}, f32[96,128]{1,0:T(8,128)S(1)}, u32[]{:S(2)}, u32[]{:S(2)}) collective-permute-start(f32[96,128]{1,0:T(8,128)S(1)} %get-tuple-element.17), channel_id=1, source_target_pairs={{0,8},{1,9},{2,10},{3,11},{4,12},{5,13},{6,14},{7,15},{8,16},{9,17... | collective-permute-start | bytes 147464 | tf_op jit(solution)/shard_map/ppermute | solution.py:597
  4.7 6.0 %copy-start.6 = (s32[1536]{0:T(1024)S(1)}, s32[1536]{0:T(1024)}, u32[]{:S(2)}) copy-start(s32[1536]{0:T(1024)} %param.12) | copy-start | bytes 18436
  4.7 8.6 %copy-start.2 = (bf16[64,96,128]{2,1,0:T(8,128)(2,1)S(1)}, bf16[64,96,128]{2,1,0:T(8,128)(2,1)}, u32[]{:S(2)}) copy-start(bf16[64,96,128]{2,1,0:T(8,128)(2,1)} %temper_hbm.1) | copy-start | bytes 4718596
  4.7 8.6 %copy-start.5 = (s32[1536,1]{0,1:T(1,128)S(1)}, s32[1536,1]{0,1:T(1,128)}, u32[]{:S(2)}) copy-start(s32[1536,1]{0,1:T(1,128)} %param.11) | copy-start | bytes 18436
  4.7 6.0 %collective-permute-start.1 = (f32[96,128]{1,0:T(8,128)S(1)}, f32[96,128]{1,0:T(8,128)S(1)}, u32[]{:S(2)}, u32[]{:S(2)}) collective-permute-start(f32[96,128]{1,0:T(8,128)S(1)} %get-tuple-element.18), channel_id=1, source_target_pairs={{0,120},{1,121},{2,122},{3,123},{4,124},{5,125},{6,126},{7,127},{8... | collective-permute-start | bytes 147464 | tf_op jit(solution)/shard_map/ppermute | solution.py:597
  10.7 4.0 %collective-permute-start.2 = (f32[64,128]{1,0:T(8,128)S(1)}, f32[64,128]{1,0:T(8,128)S(1)}, u32[]{:S(2)}, u32[]{:S(2)}) collective-permute-start(f32[64,128]{1,0:T(8,128)S(1)} %get-tuple-element.21), channel_id=1, source_target_pairs={{0,1},{1,2},{2,3},{3,4},{4,5},{5,6},{6,7},{7,0},{8,9},{9,10},{10,1... | collective-permute-start | bytes 98312 | tf_op jit(solution)/shard_map/ppermute | solution.py:597
  13.3 3.3 %collective-permute-start.3 = (f32[64,128]{1,0:T(8,128)S(1)}, f32[64,128]{1,0:T(8,128)S(1)}, u32[]{:S(2)}, u32[]{:S(2)}) collective-permute-start(f32[64,128]{1,0:T(8,128)S(1)} %get-tuple-element.22), channel_id=1, source_target_pairs={{0,7},{1,0},{2,1},{3,2},{4,3},{5,4},{6,5},{7,6},{8,15},{9,8},{10,9... | collective-permute-start | bytes 98312 | tf_op jit(solution)/shard_map/ppermute | solution.py:597
  20.7 36.6 %copy-start.3 = (bf16[256,2048]{1,0:T(8,128)(2,1)S(1)}, bf16[256,2048]{1,0:T(8,128)(2,1)}, u32[]{:S(2)}) copy-start(bf16[256,2048]{1,0:T(8,128)(2,1)} %win_ref.1) | copy-start | bytes 3145732
  20.7 36.5 %copy-start.4 = (bf16[2048,256]{1,0:T(8,128)(2,1)S(1)}, bf16[2048,256]{1,0:T(8,128)(2,1)}, u32[]{:S(2)}) copy-start(bf16[2048,256]{1,0:T(8,128)(2,1)} %wout_ref.1) | copy-start | bytes 3145732

commit v6 on v4

--- a/solution.py
+++ b/solution.py
@@ -443,7 +443,7 @@
             tracer.append(lines[:cap])
             temper.append(lines[cap : 2 * cap])
             mine += [jnp.where(lane == sub + 8 * j, lines[2 * cap :], 0.0) for j in range(cap // 8)]
-        state = -jnp.concatenate(
+        state = jnp.concatenate(
             [jnp.concatenate(tracer, axis=0), jnp.concatenate(temper, axis=0)], axis=1
         ).astype(BF16)
         mine = jnp.concatenate(mine, axis=0).astype(BF16)
@@ -466,7 +466,7 @@
             at, line = pl.ds(i * step, step), pl.ds(r, tile)
             group = i * 4 // parts
             top = jnp.concatenate([bound[group - 1, line]] * (step // lev), axis=1) if group else 120.0
-            capped = jnp.minimum(depth[line, at] * LOG2E, top)
+            capped = jnp.minimum(depth[line, at] * -LOG2E, top)
             soft = capped - jnp.log2(1.0 + jnp.exp2(capped))
             kept = jnp.exp2(soft * aerosol_ref[block, line, at].astype(F32)).astype(BF16)
             trans[line, at] = kept
@@ -506,7 +506,7 @@
 def radiate(arrived, aerosol, band_in, band_out, cap):
     lev = arrived.shape[1]
     rows, width = aerosol.shape
-    block = 16 * cap
+    block = 8 * cap
     in_vmem = pl.BlockSpec(memory_space=pltpu.VMEM)
     return call(
         functools.partial(radiate_kernel, cap),

time: 103 us -> 104 us (level)
  transfers between devices with their start and end apart: 4 -> 4, of which waited for: 1 -> 1; matrix products, arithmetic and copies ran while one was open for 0% -> 0% of each run, Pallas kernels for 4% -> 3%
where the time goes in v6:
time: 104 us
  blocking collectives  65.4 us (63%)
  Pallas kernels  27.3 us (26%)
  starting transfers between devices  8.46 us (8%)
  waiting for transfers between devices  1.82 us (2%)
    all_to_all x2, blocking collectives, exchange(): lax.all_to_all(x, ('dyn', 'col'), split_axis=0, concat_axis=0, tiled=True)  65.4 us
    pallas_call x7, Pallas kernels, call(): pl.pallas_call(kernel, out_shape=out_shape, compiler_params=pltpu.Compile...  27.3 us
    ppermute x4, starting transfers between devices, send(): return lax.ppermute(x, ('dyn', 'col'), pairs)  8.46 us
  transfers between devices with their start and end apart: 4, of which 1 were waited for; matrix products, arithmetic and copies ran while one was open for 0% of the time, Pallas kernels for 3%

profile of v6, /device:TPU:1, one launch (start us, length us, event | category | flops | bytes accessed | tf_op | source)
XLA Modules:
  0.0 103.8 jit_solution(17727104537140637933)
XLA Ops:
  0.6 0.0 copy-start
  0.6 0.0 copy-start.1
  0.6 1.9 %shard_map.96 = (f32[96,128]{1,0:T(8,128)S(1)}, f32[96,128]{1,0:T(8,128)S(1)}, f32[64,128]{1,0:T(8,128)S(1)}, f32[64,128]{1,0:T(8,128)S(1)}) custom-call(bf16[64,96,128]{2,1,0:T(8,128)(2,1)} %tracer.1, bf16[2,64,96,128]{3,2,1,0:T(8,128)(2,1)} %winds.1), custom_call_target="tpu_custom_call" | custom-call | flops 1000000 | bytes 3000000 | tf_op jit(solution)/shard_map/pallas_call | solution.py:54
  2.6 2.1 %collective-permute-start = (f32[96,128]{1,0:T(8,128)S(1)}, f32[96,128]{1,0:T(8,128)S(1)}, u32[]{:S(2)}, u32[]{:S(2)}) collective-permute-start(f32[96,128]{1,0:T(8,128)S(1)} %get-tuple-element.17), channel_id=1, source_target_pairs={{0,8},{1,9},{2,10},{3,11},{4,12},{5,13},{6,14},{7,15},{8,16},{9,17... | collective-permute-start | bytes 147464 | tf_op jit(solution)/shard_map/ppermute | solution.py:592
  4.7 0.0 copy-start.6
  4.7 0.0 copy-start.2
  4.7 0.0 copy-start.5
  4.7 3.8 %collective-permute-start.1 = (f32[96,128]{1,0:T(8,128)S(1)}, f32[96,128]{1,0:T(8,128)S(1)}, u32[]{:S(2)}, u32[]{:S(2)}) collective-permute-start(f32[96,128]{1,0:T(8,128)S(1)} %get-tuple-element.18), channel_id=1, source_target_pairs={{0,120},{1,121},{2,122},{3,123},{4,124},{5,125},{6,126},{7,127},{8... | collective-permute-start | bytes 147464 | tf_op jit(solution)/shard_map/ppermute | solution.py:592
  8.5 0.0 copy-done
  8.5 0.0 copy-done.1
  8.5 2.1 %shard_map.95 = (f32[6144,128]{1,0:T(8,128)S(1)}, f32[6144,128]{1,0:T(8,128)S(1)}) custom-call(bf16[64,96,128]{2,1,0:T(8,128)(2,1)S(1)} %copy-done.1, bf16[2,64,96,128]{3,2,1,0:T(8,128)(2,1)S(1)} %copy-done), custom_call_target="tpu_custom_call" | custom-call | flops 2000000000 | bytes 8000000 | tf_op jit(solution)/shard_map/pallas_call | solution.py:54
  10.7 0.0 copy-done.6
  10.7 0.0 collective-permute-done.xprev
  10.7 0.0 collective-permute-done.1.xnext
  10.7 2.5 %collective-permute-start.2 = (f32[64,128]{1,0:T(8,128)S(1)}, f32[64,128]{1,0:T(8,128)S(1)}, u32[]{:S(2)}, u32[]{:S(2)}) collective-permute-start(f32[64,128]{1,0:T(8,128)S(1)} %get-tuple-element.21), channel_id=1, source_target_pairs={{0,1},{1,2},{2,3},{3,4},{4,5},{5,6},{6,7},{7,0},{8,9},{9,10},{10,1... | collective-permute-start | bytes 98312 | tf_op jit(solution)/shard_map/ppermute | solution.py:592
  13.3 0.0 collective-permute-start.3
  13.3 0.0 copy-done.2
  13.3 0.0 copy-done.5
  13.3 1.5 %shard_map.98 = (s32[1,1536]{1,0:T(1,128)S(1)}, f32[128,128]{1,0:T(8,128)S(1)}, bf16[1536,128]{1,0:T(8,128)(2,1)S(1)}) custom-call(s32[1,1536]{1,0:T(1,128)S(1)} %bitcast.10, s32[1,1536]{1,0:T(1,128)S(1)} %reshape.23.classes_ref, bf16[64,96,128]{2,1,0:T(8,128)(2,1)S(1)} %copy-done.2), custom_call_target="tpu_custom_call" | custom-call | flops 1000000000 | bytes 4000000 | tf_op jit(solution)/shard_map/pallas_call | solution.py:54
  14.8 0.0 collective-permute-done.2.yprev
  14.8 1.8 %collective-permute-done.3.ynext = f32[64,128]{1,0:T(8,128)S(1)} collective-permute-done((f32[64,128]{1,0:T(8,128)S(1)}, f32[64,128]{1,0:T(8,128)S(1)}, u32[]{:S(2)}, u32[]{:S(2)}) %collective-permute-start.3) | collective-permute-done | bytes 32800 | tf_op jit(solution)/shard_map/ppermute | solution.py:592
  16.6 4.1 %shard_map.99 = (bf16[64,96,128]{2,1,0:T(8,128)(2,1)}, bf16[7168,128]{1,0:T(8,128)(2,1)S(1)}) custom-call(f32[6144,128]{1,0:T(8,128)S(1)} %get-tuple-element.15.nodes_ref, f32[6144,128]{1,0:T(8,128)S(1)} %get-tuple-element.16.tend_ref, f32[96,128]{1,0:T(8,128)S(1)} %collective-permute-done.xprev, f32[96,128]{1,0:T(8,128)S(1)} %collective-permute-done.1.xnext, ...), custom_call_target="tpu_custom_call" | custom-call | flops 4000000000 | bytes 8000000 | tf_op jit(solution)/shard_map/pallas_call | solution.py:54
  20.7 0.0 copy-start.3
  20.7 0.0 copy-start.4
  20.7 36.5 %all_to_all.10 = bf16[128,56,128]{2,1,0:T(8,128)(2,1)S(1)} all-to-all(bf16[128,56,128]{2,1,0:T(8,128)(2,1)S(1)} %bitcast.6), channel_id=1, replica_groups=mesh['dyn'=16,'col'=8] {'dyn','col'}, dimensions={0} | all-to-all | bytes 3670016 | tf_op jit(solution)/shard_map/all_to_all | solution.py:577
  57.2 0.0 copy-done.3
  57.2 0.0 copy-done.4
  57.2 13.9 %shard_map.100 = bf16[3072,256]{1,0:T(8,128)(2,1)S(1)} custom-call(bf16[7168,128]{1,0:T(8,128)(2,1)S(1)} %bitcast.7, bf16[3072,2048]{1,0:T(8,128)(2,1)} %bitcast.13, bf16[256,2048]{1,0:T(8,128)(2,1)S(1)} %copy-done.3, bf16[2048,256]{1,0:T(8,128)(2,1)S(1)} %copy-done.4), custom_call_target="tpu_custom_call" | custom-call | flops 7000000000 | bytes 20000000 | tf_op jit(solution)/shard_map/pallas_call | solution.py:54
  71.2 28.9 %all_to_all.11 = bf16[128,24,256]{2,1,0:T(8,128)(2,1)S(1)} all-to-all(bf16[128,24,256]{2,1,0:T(8,128)(2,1)S(1)} %bitcast.9), channel_id=1, replica_groups=mesh['dyn'=16,'col'=8] {'dyn','col'}, dimensions={0} | all-to-all | bytes 3145728 | tf_op jit(solution)/shard_map/all_to_all | solution.py:577
  100.1 3.7 %shard_map.101 = bf16[1536,256]{1,0:T(8,128)(2,1)} custom-call(s32[1,1536]{1,0:T(1,128)S(1)} %bitcast.12, s32[1,1536]{1,0:T(1,128)S(1)} %get-tuple-element.23.slot_ref, bf16[3072,256]{1,0:T(8,128)(2,1)S(1)} %bitcast.8), custom_call_target="tpu_custom_call" | custom-call | flops 3000000000 | bytes 3000000 | tf_op jit(solution)/shard_map/pallas_call | solution.py:54
  (2 shorter events, 0.0 us)
Async XLA Ops:
  0.6 7.9 %copy-start = (bf16[2,64,96,128]{3,2,1,0:T(8,128)(2,1)S(1)}, bf16[2,64,96,128]{3,2,1,0:T(8,128)(2,1)}, u32[]{:S(2)}) copy-start(bf16[2,64,96,128]{3,2,1,0:T(8,128)(2,1)} %winds.1) | copy-start | bytes 9437188
  0.6 7.9 %copy-start.1 = (bf16[64,96,128]{2,1,0:T(8,128)(2,1)S(1)}, bf16[64,96,128]{2,1,0:T(8,128)(2,1)}, u32[]{:S(2)}) copy-start(bf16[64,96,128]{2,1,0:T(8,128)(2,1)} %tracer.1) | copy-start | bytes 4718596
  2.6 8.1 %collective-permute-start = (f32[96,128]{1,0:T(8,128)S(1)}, f32[96,128]{1,0:T(8,128)S(1)}, u32[]{:S(2)}, u32[]{:S(2)}) collective-permute-start(f32[96,128]{1,0:T(8,128)S(1)} %get-tuple-element.17), channel_id=1, source_target_pairs={{0,8},{1,9},{2,10},{3,11},{4,12},{5,13},{6,14},{7,15},{8,16},{9,17... | collective-permute-start | bytes 147464 | tf_op jit(solution)/shard_map/ppermute | solution.py:592
  4.7 6.0 %copy-start.6 = (s32[1536]{0:T(1024)S(1)}, s32[1536]{0:T(1024)}, u32[]{:S(2)}) copy-start(s32[1536]{0:T(1024)} %param.12) | copy-start | bytes 18436
  4.7 8.6 %copy-start.2 = (bf16[64,96,128]{2,1,0:T(8,128)(2,1)S(1)}, bf16[64,96,128]{2,1,0:T(8,128)(2,1)}, u32[]{:S(2)}) copy-start(bf16[64,96,128]{2,1,0:T(8,128)(2,1)} %temper_hbm.1) | copy-start | bytes 4718596
  4.7 8.6 %copy-start.5 = (s32[1536,1]{0,1:T(1,128)S(1)}, s32[1536,1]{0,1:T(1,128)}, u32[]{:S(2)}) copy-start(s32[1536,1]{0,1:T(1,128)} %param.11) | copy-start | bytes 18436
  4.7 6.0 %collective-permute-start.1 = (f32[96,128]{1,0:T(8,128)S(1)}, f32[96,128]{1,0:T(8,128)S(1)}, u32[]{:S(2)}, u32[]{:S(2)}) collective-permute-start(f32[96,128]{1,0:T(8,128)S(1)} %get-tuple-element.18), channel_id=1, source_target_pairs={{0,120},{1,121},{2,122},{3,123},{4,124},{5,125},{6,126},{7,127},{8... | collective-permute-start | bytes 147464 | tf_op jit(solution)/shard_map/ppermute | solution.py:592
  10.7 4.0 %collective-permute-start.2 = (f32[64,128]{1,0:T(8,128)S(1)}, f32[64,128]{1,0:T(8,128)S(1)}, u32[]{:S(2)}, u32[]{:S(2)}) collective-permute-start(f32[64,128]{1,0:T(8,128)S(1)} %get-tuple-element.21), channel_id=1, source_target_pairs={{0,1},{1,2},{2,3},{3,4},{4,5},{5,6},{6,7},{7,0},{8,9},{9,10},{10,1... | collective-permute-start | bytes 98312 | tf_op jit(solution)/shard_map/ppermute | solution.py:592
  13.3 3.3 %collective-permute-start.3 = (f32[64,128]{1,0:T(8,128)S(1)}, f32[64,128]{1,0:T(8,128)S(1)}, u32[]{:S(2)}, u32[]{:S(2)}) collective-permute-start(f32[64,128]{1,0:T(8,128)S(1)} %get-tuple-element.22), channel_id=1, source_target_pairs={{0,7},{1,0},{2,1},{3,2},{4,3},{5,4},{6,5},{7,6},{8,15},{9,8},{10,9... | collective-permute-start | bytes 98312 | tf_op jit(solution)/shard_map/ppermute | solution.py:592
  20.7 36.5 %copy-start.3 = (bf16[256,2048]{1,0:T(8,128)(2,1)S(1)}, bf16[256,2048]{1,0:T(8,128)(2,1)}, u32[]{:S(2)}) copy-start(bf16[256,2048]{1,0:T(8,128)(2,1)} %win_ref.1) | copy-start | bytes 3145732
  20.7 36.5 %copy-start.4 = (bf16[2048,256]{1,0:T(8,128)(2,1)S(1)}, bf16[2048,256]{1,0:T(8,128)(2,1)}, u32[]{:S(2)}) copy-start(bf16[2048,256]{1,0:T(8,128)(2,1)} %wout_ref.1) | copy-start | bytes 3145732

commit v7 on v5

--- a/solution.py
+++ b/solution.py
@@ -443,7 +443,7 @@
             tracer.append(lines[:cap])
             temper.append(lines[cap : 2 * cap])
             mine += [jnp.where(lane == sub + 8 * j, lines[2 * cap :], 0.0) for j in range(cap // 8)]
-        state = -jnp.concatenate(
+        state = jnp.concatenate(
             [jnp.concatenate(tracer, axis=0), jnp.concatenate(temper, axis=0)], axis=1
         ).astype(BF16)
         mine = jnp.concatenate(mine, axis=0).astype(BF16)
@@ -458,7 +458,7 @@
         at = pl.ds(h * half, half)
         depth[:, at] = jnp.dot(state, win_ref[:, at], preferred_element_type=F32)
 
-    step, tile = 256, 64
+    step, tile = 256, 128
     parts = width // step
 
     def middle(block, depth, bound, trans, chunks):
@@ -466,7 +466,7 @@
             at, line = pl.ds(i * step, step), pl.ds(r, tile)
             group = i * 4 // parts
             top = jnp.concatenate([bound[group - 1, line]] * (step // lev), axis=1) if group else 120.0
-            capped = jnp.minimum(depth[line, at] * LOG2E, top)
+            capped = jnp.minimum(depth[line, at] * -LOG2E, top)
             soft = capped - jnp.log2(1.0 + jnp.exp2(capped))
             kept = jnp.exp2(soft * aerosol_ref[block, line, at].astype(F32)).astype(BF16)
             trans[line, at] = kept

time: 103 us -> 104 us (level)
  no operation moved by 1% of the time
where the time goes in v7:
time: 104 us; the launch traced here: 103 us
  blocking collectives  65.4 us (63%)
  Pallas kernels  26.8 us (26%)
  starting transfers between devices  8.46 us (8%)
  waiting for transfers between devices  1.82 us (2%)
    all_to_all x2, blocking collectives, exchange(): lax.all_to_all(x, ('dyn', 'col'), split_axis=0, concat_axis=0, tiled=True)  65.4 us
    pallas_call x7, Pallas kernels, call(): pl.pallas_call(kernel, out_shape=out_shape, compiler_params=pltpu.Compile...  26.8 us
    ppermute x4, starting transfers between devices, send(): return lax.ppermute(x, ('dyn', 'col'), pairs)  8.46 us
  transfers between devices with their start and end apart: 4, of which 1 were waited for; matrix products, arithmetic and copies ran while one was open for 0% of the time, Pallas kernels for 4%

profile of v7, /device:TPU:1, one launch (start us, length us, event | category | flops | bytes accessed | tf_op | source)
XLA Modules:
  0.0 103.5 jit_solution(5431532529528948517)
XLA Ops:
  0.6 0.0 copy-start
  0.6 0.0 copy-start.1
  0.6 1.9 %shard_map.96 = (f32[96,128]{1,0:T(8,128)S(1)}, f32[96,128]{1,0:T(8,128)S(1)}, f32[64,128]{1,0:T(8,128)S(1)}, f32[64,128]{1,0:T(8,128)S(1)}) custom-call(bf16[64,96,128]{2,1,0:T(8,128)(2,1)} %tracer.1, bf16[2,64,96,128]{3,2,1,0:T(8,128)(2,1)} %winds.1), custom_call_target="tpu_custom_call" | custom-call | flops 1000000 | bytes 3000000 | tf_op jit(solution)/shard_map/pallas_call | solution.py:54
  2.6 2.1 %collective-permute-start = (f32[96,128]{1,0:T(8,128)S(1)}, f32[96,128]{1,0:T(8,128)S(1)}, u32[]{:S(2)}, u32[]{:S(2)}) collective-permute-start(f32[96,128]{1,0:T(8,128)S(1)} %get-tuple-element.17), channel_id=1, source_target_pairs={{0,8},{1,9},{2,10},{3,11},{4,12},{5,13},{6,14},{7,15},{8,16},{9,17... | collective-permute-start | bytes 147464 | tf_op jit(solution)/shard_map/ppermute | solution.py:597
  4.7 0.0 copy-start.6
  4.7 0.0 copy-start.2
  4.7 0.0 copy-start.5
  4.7 3.8 %collective-permute-start.1 = (f32[96,128]{1,0:T(8,128)S(1)}, f32[96,128]{1,0:T(8,128)S(1)}, u32[]{:S(2)}, u32[]{:S(2)}) collective-permute-start(f32[96,128]{1,0:T(8,128)S(1)} %get-tuple-element.18), channel_id=1, source_target_pairs={{0,120},{1,121},{2,122},{3,123},{4,124},{5,125},{6,126},{7,127},{8... | collective-permute-start | bytes 147464 | tf_op jit(solution)/shard_map/ppermute | solution.py:597
  8.5 0.0 copy-done
  8.5 0.0 copy-done.1
  8.5 2.1 %shard_map.95 = (f32[6144,128]{1,0:T(8,128)S(1)}, f32[6144,128]{1,0:T(8,128)S(1)}) custom-call(bf16[64,96,128]{2,1,0:T(8,128)(2,1)S(1)} %copy-done.1, bf16[2,64,96,128]{3,2,1,0:T(8,128)(2,1)S(1)} %copy-done), custom_call_target="tpu_custom_call" | custom-call | flops 2000000000 | bytes 8000000 | tf_op jit(solution)/shard_map/pallas_call | solution.py:54
  10.7 0.0 copy-done.6
  10.7 0.0 collective-permute-done.xprev
  10.7 0.0 collective-permute-done.1.xnext
  10.7 2.5 %collective-permute-start.2 = (f32[64,128]{1,0:T(8,128)S(1)}, f32[64,128]{1,0:T(8,128)S(1)}, u32[]{:S(2)}, u32[]{:S(2)}) collective-permute-start(f32[64,128]{1,0:T(8,128)S(1)} %get-tuple-element.21), channel_id=1, source_target_pairs={{0,1},{1,2},{2,3},{3,4},{4,5},{5,6},{6,7},{7,0},{8,9},{9,10},{10,1... | collective-permute-start | bytes 98312 | tf_op jit(solution)/shard_map/ppermute | solution.py:597
  13.3 0.0 collective-permute-start.3
  13.3 0.0 copy-done.2
  13.3 0.0 copy-done.5
  13.3 1.5 %shard_map.98 = (s32[1,1536]{1,0:T(1,128)S(1)}, f32[128,128]{1,0:T(8,128)S(1)}, bf16[1536,128]{1,0:T(8,128)(2,1)S(1)}) custom-call(s32[1,1536]{1,0:T(1,128)S(1)} %bitcast.10, s32[1,1536]{1,0:T(1,128)S(1)} %reshape.23.classes_ref, bf16[64,96,128]{2,1,0:T(8,128)(2,1)S(1)} %copy-done.2), custom_call_target="tpu_custom_call" | custom-call | flops 1000000000 | bytes 4000000 | tf_op jit(solution)/shard_map/pallas_call | solution.py:54
  14.8 0.0 collective-permute-done.2.yprev
  14.8 1.8 %collective-permute-done.3.ynext = f32[64,128]{1,0:T(8,128)S(1)} collective-permute-done((f32[64,128]{1,0:T(8,128)S(1)}, f32[64,128]{1,0:T(8,128)S(1)}, u32[]{:S(2)}, u32[]{:S(2)}) %collective-permute-start.3) | collective-permute-done | bytes 32800 | tf_op jit(solution)/shard_map/ppermute | solution.py:597
  16.6 4.1 %shard_map.99 = (bf16[64,96,128]{2,1,0:T(8,128)(2,1)}, bf16[7168,128]{1,0:T(8,128)(2,1)S(1)}) custom-call(f32[6144,128]{1,0:T(8,128)S(1)} %get-tuple-element.15.nodes_ref, f32[6144,128]{1,0:T(8,128)S(1)} %get-tuple-element.16.tend_ref, f32[96,128]{1,0:T(8,128)S(1)} %collective-permute-done.xprev, f32[96,128]{1,0:T(8,128)S(1)} %collective-permute-done.1.xnext, ...), custom_call_target="tpu_custom_call" | custom-call | flops 4000000000 | bytes 8000000 | tf_op jit(solution)/shard_map/pallas_call | solution.py:54
  20.7 0.0 copy-start.3
  20.7 0.0 copy-start.4
  20.7 36.5 %all_to_all.10 = bf16[128,56,128]{2,1,0:T(8,128)(2,1)S(1)} all-to-all(bf16[128,56,128]{2,1,0:T(8,128)(2,1)S(1)} %bitcast.6), channel_id=1, replica_groups=mesh['dyn'=16,'col'=8] {'dyn','col'}, dimensions={0} | all-to-all | bytes 3670016 | tf_op jit(solution)/shard_map/all_to_all | solution.py:582
  57.2 0.0 copy-done.3
  57.2 0.0 copy-done.4
  57.2 13.4 %shard_map.100 = bf16[3072,256]{1,0:T(8,128)(2,1)S(1)} custom-call(bf16[7168,128]{1,0:T(8,128)(2,1)S(1)} %bitcast.7, bf16[3072,2048]{1,0:T(8,128)(2,1)} %bitcast.13, bf16[256,2048]{1,0:T(8,128)(2,1)S(1)} %copy-done.3, bf16[2048,256]{1,0:T(8,128)(2,1)S(1)} %copy-done.4), custom_call_target="tpu_custom_call" | custom-call | flops 7000000000 | bytes 20000000 | tf_op jit(solution)/shard_map/pallas_call | solution.py:54
  70.7 28.9 %all_to_all.11 = bf16[128,24,256]{2,1,0:T(8,128)(2,1)S(1)} all-to-all(bf16[128,24,256]{2,1,0:T(8,128)(2,1)S(1)} %bitcast.9), channel_id=1, replica_groups=mesh['dyn'=16,'col'=8] {'dyn','col'}, dimensions={0} | all-to-all | bytes 3145728 | tf_op jit(solution)/shard_map/all_to_all | solution.py:582
  99.6 3.7 %shard_map.101 = bf16[1536,256]{1,0:T(8,128)(2,1)} custom-call(s32[1,1536]{1,0:T(1,128)S(1)} %bitcast.12, s32[1,1536]{1,0:T(1,128)S(1)} %get-tuple-element.23.slot_ref, bf16[3072,256]{1,0:T(8,128)(2,1)S(1)} %bitcast.8), custom_call_target="tpu_custom_call" | custom-call | flops 3000000000 | bytes 3000000 | tf_op jit(solution)/shard_map/pallas_call | solution.py:54
  (2 shorter events, 0.0 us)
Async XLA Ops:
  0.6 7.9 %copy-start = (bf16[2,64,96,128]{3,2,1,0:T(8,128)(2,1)S(1)}, bf16[2,64,96,128]{3,2,1,0:T(8,128)(2,1)}, u32[]{:S(2)}) copy-start(bf16[2,64,96,128]{3,2,1,0:T(8,128)(2,1)} %winds.1) | copy-start | bytes 9437188
  0.6 7.9 %copy-start.1 = (bf16[64,96,128]{2,1,0:T(8,128)(2,1)S(1)}, bf16[64,96,128]{2,1,0:T(8,128)(2,1)}, u32[]{:S(2)}) copy-start(bf16[64,96,128]{2,1,0:T(8,128)(2,1)} %tracer.1) | copy-start | bytes 4718596
  2.6 8.1 %collective-permute-start = (f32[96,128]{1,0:T(8,128)S(1)}, f32[96,128]{1,0:T(8,128)S(1)}, u32[]{:S(2)}, u32[]{:S(2)}) collective-permute-start(f32[96,128]{1,0:T(8,128)S(1)} %get-tuple-element.17), channel_id=1, source_target_pairs={{0,8},{1,9},{2,10},{3,11},{4,12},{5,13},{6,14},{7,15},{8,16},{9,17... | collective-permute-start | bytes 147464 | tf_op jit(solution)/shard_map/ppermute | solution.py:597
  4.7 6.0 %copy-start.6 = (s32[1536]{0:T(1024)S(1)}, s32[1536]{0:T(1024)}, u32[]{:S(2)}) copy-start(s32[1536]{0:T(1024)} %param.12) | copy-start | bytes 18436
  4.7 8.6 %copy-start.2 = (bf16[64,96,128]{2,1,0:T(8,128)(2,1)S(1)}, bf16[64,96,128]{2,1,0:T(8,128)(2,1)}, u32[]{:S(2)}) copy-start(bf16[64,96,128]{2,1,0:T(8,128)(2,1)} %temper_hbm.1) | copy-start | bytes 4718596
  4.7 8.6 %copy-start.5 = (s32[1536,1]{0,1:T(1,128)S(1)}, s32[1536,1]{0,1:T(1,128)}, u32[]{:S(2)}) copy-start(s32[1536,1]{0,1:T(1,128)} %param.11) | copy-start | bytes 18436
  4.7 6.0 %collective-permute-start.1 = (f32[96,128]{1,0:T(8,128)S(1)}, f32[96,128]{1,0:T(8,128)S(1)}, u32[]{:S(2)}, u32[]{:S(2)}) collective-permute-start(f32[96,128]{1,0:T(8,128)S(1)} %get-tuple-element.18), channel_id=1, source_target_pairs={{0,120},{1,121},{2,122},{3,123},{4,124},{5,125},{6,126},{7,127},{8... | collective-permute-start | bytes 147464 | tf_op jit(solution)/shard_map/ppermute | solution.py:597
  10.7 4.0 %collective-permute-start.2 = (f32[64,128]{1,0:T(8,128)S(1)}, f32[64,128]{1,0:T(8,128)S(1)}, u32[]{:S(2)}, u32[]{:S(2)}) collective-permute-start(f32[64,128]{1,0:T(8,128)S(1)} %get-tuple-element.21), channel_id=1, source_target_pairs={{0,1},{1,2},{2,3},{3,4},{4,5},{5,6},{6,7},{7,0},{8,9},{9,10},{10,1... | collective-permute-start | bytes 98312 | tf_op jit(solution)/shard_map/ppermute | solution.py:597
  13.3 3.3 %collective-permute-start.3 = (f32[64,128]{1,0:T(8,128)S(1)}, f32[64,128]{1,0:T(8,128)S(1)}, u32[]{:S(2)}, u32[]{:S(2)}) collective-permute-start(f32[64,128]{1,0:T(8,128)S(1)} %get-tuple-element.22), channel_id=1, source_target_pairs={{0,7},{1,0},{2,1},{3,2},{4,3},{5,4},{6,5},{7,6},{8,15},{9,8},{10,9... | collective-permute-start | bytes 98312 | tf_op jit(solution)/shard_map/ppermute | solution.py:597
  20.7 36.6 %copy-start.3 = (bf16[256,2048]{1,0:T(8,128)(2,1)S(1)}, bf16[256,2048]{1,0:T(8,128)(2,1)}, u32[]{:S(2)}) copy-start(bf16[256,2048]{1,0:T(8,128)(2,1)} %win_ref.1) | copy-start | bytes 3145732
  20.7 36.5 %copy-start.4 = (bf16[2048,256]{1,0:T(8,128)(2,1)S(1)}, bf16[2048,256]{1,0:T(8,128)(2,1)}, u32[]{:S(2)}) copy-start(bf16[2048,256]{1,0:T(8,128)(2,1)} %wout_ref.1) | copy-start | bytes 3145732

commit v8 on v7

--- a/solution.py
+++ b/solution.py
@@ -458,7 +458,7 @@
         at = pl.ds(h * half, half)
         depth[:, at] = jnp.dot(state, win_ref[:, at], preferred_element_type=F32)
 
-    step, tile = 256, 128
+    step, tile = 256, 32
     parts = width // step
 
     def middle(block, depth, bound, trans, chunks):

time: 104 us -> 103 us (level)
  no operation moved by 1% of the time
where the time goes in v8:
time: 103 us
  blocking collectives  65.4 us (63%)
  Pallas kernels  26.2 us (25%)
  starting transfers between devices  8.46 us (8%)
  waiting for transfers between devices  1.82 us (2%)
    all_to_all x2, blocking collectives, exchange(): lax.all_to_all(x, ('dyn', 'col'), split_axis=0, concat_axis=0, tiled=True)  65.4 us
    pallas_call x7, Pallas kernels, call(): pl.pallas_call(kernel, out_shape=out_shape, compiler_params=pltpu.Compile...  26.2 us
    ppermute x4, starting transfers between devices, send(): return lax.ppermute(x, ('dyn', 'col'), pairs)  8.46 us
  transfers between devices with their start and end apart: 4, of which 1 were waited for; matrix products, arithmetic and copies ran while one was open for 0% of the time, Pallas kernels for 4%

profile of v8, /device:TPU:1, one launch (start us, length us, event | category | flops | bytes accessed | tf_op | source)
XLA Modules:
  0.0 102.9 jit_solution(12505758813113650691)
XLA Ops:
  0.6 0.0 copy-start
  0.6 0.0 copy-start.1
  0.6 1.9 %shard_map.96 = (f32[96,128]{1,0:T(8,128)S(1)}, f32[96,128]{1,0:T(8,128)S(1)}, f32[64,128]{1,0:T(8,128)S(1)}, f32[64,128]{1,0:T(8,128)S(1)}) custom-call(bf16[64,96,128]{2,1,0:T(8,128)(2,1)} %tracer.1, bf16[2,64,96,128]{3,2,1,0:T(8,128)(2,1)} %winds.1), custom_call_target="tpu_custom_call" | custom-call | flops 1000000 | bytes 3000000 | tf_op jit(solution)/shard_map/pallas_call | solution.py:54
  2.6 2.1 %collective-permute-start = (f32[96,128]{1,0:T(8,128)S(1)}, f32[96,128]{1,0:T(8,128)S(1)}, u32[]{:S(2)}, u32[]{:S(2)}) collective-permute-start(f32[96,128]{1,0:T(8,128)S(1)} %get-tuple-element.17), channel_id=1, source_target_pairs={{0,8},{1,9},{2,10},{3,11},{4,12},{5,13},{6,14},{7,15},{8,16},{9,17... | collective-permute-start | bytes 147464 | tf_op jit(solution)/shard_map/ppermute | solution.py:597
  4.7 0.0 copy-start.6
  4.7 0.0 copy-start.2
  4.7 0.0 copy-start.5
  4.7 3.8 %collective-permute-start.1 = (f32[96,128]{1,0:T(8,128)S(1)}, f32[96,128]{1,0:T(8,128)S(1)}, u32[]{:S(2)}, u32[]{:S(2)}) collective-permute-start(f32[96,128]{1,0:T(8,128)S(1)} %get-tuple-element.18), channel_id=1, source_target_pairs={{0,120},{1,121},{2,122},{3,123},{4,124},{5,125},{6,126},{7,127},{8... | collective-permute-start | bytes 147464 | tf_op jit(solution)/shard_map/ppermute | solution.py:597
  8.5 0.0 copy-done
  8.5 0.0 copy-done.1
  8.5 2.1 %shard_map.95 = (f32[6144,128]{1,0:T(8,128)S(1)}, f32[6144,128]{1,0:T(8,128)S(1)}) custom-call(bf16[64,96,128]{2,1,0:T(8,128)(2,1)S(1)} %copy-done.1, bf16[2,64,96,128]{3,2,1,0:T(8,128)(2,1)S(1)} %copy-done), custom_call_target="tpu_custom_call" | custom-call | flops 2000000000 | bytes 8000000 | tf_op jit(solution)/shard_map/pallas_call | solution.py:54
  10.7 0.0 copy-done.6
  10.7 0.0 collective-permute-done.xprev
  10.7 0.0 collective-permute-done.1.xnext
  10.7 2.5 %collective-permute-start.2 = (f32[64,128]{1,0:T(8,128)S(1)}, f32[64,128]{1,0:T(8,128)S(1)}, u32[]{:S(2)}, u32[]{:S(2)}) collective-permute-start(f32[64,128]{1,0:T(8,128)S(1)} %get-tuple-element.21), channel_id=1, source_target_pairs={{0,1},{1,2},{2,3},{3,4},{4,5},{5,6},{6,7},{7,0},{8,9},{9,10},{10,1... | collective-permute-start | bytes 98312 | tf_op jit(solution)/shard_map/ppermute | solution.py:597
  13.3 0.0 collective-permute-start.3
  13.3 0.0 copy-done.2
  13.3 0.0 copy-done.5
  13.3 1.5 %shard_map.98 = (s32[1,1536]{1,0:T(1,128)S(1)}, f32[128,128]{1,0:T(8,128)S(1)}, bf16[1536,128]{1,0:T(8,128)(2,1)S(1)}) custom-call(s32[1,1536]{1,0:T(1,128)S(1)} %bitcast.10, s32[1,1536]{1,0:T(1,128)S(1)} %reshape.23.classes_ref, bf16[64,96,128]{2,1,0:T(8,128)(2,1)S(1)} %copy-done.2), custom_call_target="tpu_custom_call" | custom-call | flops 1000000000 | bytes 4000000 | tf_op jit(solution)/shard_map/pallas_call | solution.py:54
  14.8 0.0 collective-permute-done.2.yprev
  14.8 1.8 %collective-permute-done.3.ynext = f32[64,128]{1,0:T(8,128)S(1)} collective-permute-done((f32[64,128]{1,0:T(8,128)S(1)}, f32[64,128]{1,0:T(8,128)S(1)}, u32[]{:S(2)}, u32[]{:S(2)}) %collective-permute-start.3) | collective-permute-done | bytes 32800 | tf_op jit(solution)/shard_map/ppermute | solution.py:597
  16.6 4.1 %shard_map.99 = (bf16[64,96,128]{2,1,0:T(8,128)(2,1)}, bf16[7168,128]{1,0:T(8,128)(2,1)S(1)}) custom-call(f32[6144,128]{1,0:T(8,128)S(1)} %get-tuple-element.15.nodes_ref, f32[6144,128]{1,0:T(8,128)S(1)} %get-tuple-element.16.tend_ref, f32[96,128]{1,0:T(8,128)S(1)} %collective-permute-done.xprev, f32[96,128]{1,0:T(8,128)S(1)} %collective-permute-done.1.xnext, ...), custom_call_target="tpu_custom_call" | custom-call | flops 4000000000 | bytes 8000000 | tf_op jit(solution)/shard_map/pallas_call | solution.py:54
  20.7 0.0 copy-start.3
  20.7 0.0 copy-start.4
  20.7 36.5 %all_to_all.10 = bf16[128,56,128]{2,1,0:T(8,128)(2,1)S(1)} all-to-all(bf16[128,56,128]{2,1,0:T(8,128)(2,1)S(1)} %bitcast.6), channel_id=1, replica_groups=mesh['dyn'=16,'col'=8] {'dyn','col'}, dimensions={0} | all-to-all | bytes 3670016 | tf_op jit(solution)/shard_map/all_to_all | solution.py:582
  57.2 0.0 copy-done.3
  57.2 0.0 copy-done.4
  57.2 12.8 %shard_map.100 = bf16[3072,256]{1,0:T(8,128)(2,1)S(1)} custom-call(bf16[7168,128]{1,0:T(8,128)(2,1)S(1)} %bitcast.7, bf16[3072,2048]{1,0:T(8,128)(2,1)} %bitcast.13, bf16[256,2048]{1,0:T(8,128)(2,1)S(1)} %copy-done.3, bf16[2048,256]{1,0:T(8,128)(2,1)S(1)} %copy-done.4), custom_call_target="tpu_custom_call" | custom-call | flops 7000000000 | bytes 20000000 | tf_op jit(solution)/shard_map/pallas_call | solution.py:54
  70.1 28.9 %all_to_all.11 = bf16[128,24,256]{2,1,0:T(8,128)(2,1)S(1)} all-to-all(bf16[128,24,256]{2,1,0:T(8,128)(2,1)S(1)} %bitcast.9), channel_id=1, replica_groups=mesh['dyn'=16,'col'=8] {'dyn','col'}, dimensions={0} | all-to-all | bytes 3145728 | tf_op jit(solution)/shard_map/all_to_all | solution.py:582
  99.0 3.7 %shard_map.101 = bf16[1536,256]{1,0:T(8,128)(2,1)} custom-call(s32[1,1536]{1,0:T(1,128)S(1)} %bitcast.12, s32[1,1536]{1,0:T(1,128)S(1)} %get-tuple-element.23.slot_ref, bf16[3072,256]{1,0:T(8,128)(2,1)S(1)} %bitcast.8), custom_call_target="tpu_custom_call" | custom-call | flops 3000000000 | bytes 3000000 | tf_op jit(solution)/shard_map/pallas_call | solution.py:54
  (2 shorter events, 0.0 us)
Async XLA Ops:
  0.6 7.9 %copy-start = (bf16[2,64,96,128]{3,2,1,0:T(8,128)(2,1)S(1)}, bf16[2,64,96,128]{3,2,1,0:T(8,128)(2,1)}, u32[]{:S(2)}) copy-start(bf16[2,64,96,128]{3,2,1,0:T(8,128)(2,1)} %winds.1) | copy-start | bytes 9437188
  0.6 7.9 %copy-start.1 = (bf16[64,96,128]{2,1,0:T(8,128)(2,1)S(1)}, bf16[64,96,128]{2,1,0:T(8,128)(2,1)}, u32[]{:S(2)}) copy-start(bf16[64,96,128]{2,1,0:T(8,128)(2,1)} %tracer.1) | copy-start | bytes 4718596
  2.6 8.1 %collective-permute-start = (f32[96,128]{1,0:T(8,128)S(1)}, f32[96,128]{1,0:T(8,128)S(1)}, u32[]{:S(2)}, u32[]{:S(2)}) collective-permute-start(f32[96,128]{1,0:T(8,128)S(1)} %get-tuple-element.17), channel_id=1, source_target_pairs={{0,8},{1,9},{2,10},{3,11},{4,12},{5,13},{6,14},{7,15},{8,16},{9,17... | collective-permute-start | bytes 147464 | tf_op jit(solution)/shard_map/ppermute | solution.py:597
  4.7 6.0 %copy-start.6 = (s32[1536]{0:T(1024)S(1)}, s32[1536]{0:T(1024)}, u32[]{:S(2)}) copy-start(s32[1536]{0:T(1024)} %param.12) | copy-start | bytes 18436
  4.7 8.6 %copy-start.2 = (bf16[64,96,128]{2,1,0:T(8,128)(2,1)S(1)}, bf16[64,96,128]{2,1,0:T(8,128)(2,1)}, u32[]{:S(2)}) copy-start(bf16[64,96,128]{2,1,0:T(8,128)(2,1)} %temper_hbm.1) | copy-start | bytes 4718596
  4.7 8.6 %copy-start.5 = (s32[1536,1]{0,1:T(1,128)S(1)}, s32[1536,1]{0,1:T(1,128)}, u32[]{:S(2)}) copy-start(s32[1536,1]{0,1:T(1,128)} %param.11) | copy-start | bytes 18436
  4.7 6.0 %collective-permute-start.1 = (f32[96,128]{1,0:T(8,128)S(1)}, f32[96,128]{1,0:T(8,128)S(1)}, u32[]{:S(2)}, u32[]{:S(2)}) collective-permute-start(f32[96,128]{1,0:T(8,128)S(1)} %get-tuple-element.18), channel_id=1, source_target_pairs={{0,120},{1,121},{2,122},{3,123},{4,124},{5,125},{6,126},{7,127},{8... | collective-permute-start | bytes 147464 | tf_op jit(solution)/shard_map/ppermute | solution.py:597
  10.7 4.0 %collective-permute-start.2 = (f32[64,128]{1,0:T(8,128)S(1)}, f32[64,128]{1,0:T(8,128)S(1)}, u32[]{:S(2)}, u32[]{:S(2)}) collective-permute-start(f32[64,128]{1,0:T(8,128)S(1)} %get-tuple-element.21), channel_id=1, source_target_pairs={{0,1},{1,2},{2,3},{3,4},{4,5},{5,6},{6,7},{7,0},{8,9},{9,10},{10,1... | collective-permute-start | bytes 98312 | tf_op jit(solution)/shard_map/ppermute | solution.py:597
  13.3 3.3 %collective-permute-start.3 = (f32[64,128]{1,0:T(8,128)S(1)}, f32[64,128]{1,0:T(8,128)S(1)}, u32[]{:S(2)}, u32[]{:S(2)}) collective-permute-start(f32[64,128]{1,0:T(8,128)S(1)} %get-tuple-element.22), channel_id=1, source_target_pairs={{0,7},{1,0},{2,1},{3,2},{4,3},{5,4},{6,5},{7,6},{8,15},{9,8},{10,9... | collective-permute-start | bytes 98312 | tf_op jit(solution)/shard_map/ppermute | solution.py:597
  20.7 36.6 %copy-start.3 = (bf16[256,2048]{1,0:T(8,128)(2,1)S(1)}, bf16[256,2048]{1,0:T(8,128)(2,1)}, u32[]{:S(2)}) copy-start(bf16[256,2048]{1,0:T(8,128)(2,1)} %win_ref.1) | copy-start | bytes 3145732
  20.7 36.5 %copy-start.4 = (bf16[2048,256]{1,0:T(8,128)(2,1)S(1)}, bf16[2048,256]{1,0:T(8,128)(2,1)}, u32[]{:S(2)}) copy-start(bf16[2048,256]{1,0:T(8,128)(2,1)} %wout_ref.1) | copy-start | bytes 3145732
